TPU v7x, 32 devices: a whole 2x2x4 slice. The times are simulated.
32 devices in a mesh: dp: 8 (over y, x, core), pix: 4 (over z).
Axes of the slice: x: 2, y: 2, z: 4, core: 2. Of those that a mesh axis runs over, the one named last changes fastest.
Arguments:
- latents: bfloat16 [512, 1024], replicated, may hold values from -6 to 6
- pixel_rgb: bfloat16 [3, 131072], P(None, ('dp', 'pix')), may hold values from -1 to 1
- coords: int32 [2, 131072], P(None, ('dp', 'pix')), may hold values from 0 to 111, as said below
- segment_ids: int32 [131072], P(('dp', 'pix')), may hold values from 0 to 4, as said below
- image_sizes: int32 [2, 32], P(None, 'dp'), may hold values from 16 to 112, as said below
- input_gain: float32 [261], replicated, may hold values from 0.5 to 1.5
- input_bias: float32 [261], replicated, may hold values from -1 to 1
- query_weight: bfloat16 [1024, 1024], replicated, may hold values from -0.375 to 0.375
- query_bias: float32 [1024], replicated, may hold values from -2.5 to 2.5
- key_weight: bfloat16 [261, 1024], replicated, may hold values from -0.375 to 0.375
- value_weight: bfloat16 [261, 1024], replicated, may hold values from -0.375 to 0.375
- value_bias: float32 [1024], replicated, may hold values from -1.5 to 1.5
- out_weight: bfloat16 [1024, 1024], replicated, may hold values from -1 to 1
- out_bias: float32 [1024], replicated, may hold values from -1.5 to 1.5
- latent_gain: float32 [1024], replicated, may hold values from 0.5 to 1.5
- latent_bias: float32 [1024], replicated, may hold values from -1 to 1
- mlp_gain: float32 [1024], replicated, may hold values from 0.5 to 1.5
- mlp_bias: float32 [1024], replicated, may hold values from -1 to 1
- up_weight: bfloat16 [1024, 1024], replicated, may hold values from -0.1875 to 0.1875
- up_bias: float32 [1024], replicated, may hold values from -1.5 to 1.5
- down_weight: bfloat16 [1024, 1024], replicated, may hold values from -0.1875 to 0.1875
- down_bias: float32 [1024], replicated, may hold values from -1.5 to 1.5
- cotangent: float32 [32, 512, 1024], P(('dp', 'pix')), may hold values from -6 to 6
Outputs:
- latents_out: float32 [32, 512, 1024], P(('dp', 'pix'))
- rgb_grad: bfloat16 [3, 131072], P(None, ('dp', 'pix'))
- latents_grad: float32 [512, 1024], P('pix', 'dp')
- query_weight_grad: float32 [1024, 1024], P('pix', 'dp')
- query_bias_grad: float32 [1024], replicated
- key_weight_grad: float32 [261, 1024], replicated
- value_weight_grad: float32 [261, 1024], replicated
- value_bias_grad: float32 [1024], replicated
- out_weight_grad: float32 [1024, 1024], P('pix', 'dp')
- out_bias_grad: float32 [1024], replicated
- latent_gain_grad: float32 [1024], replicated
- latent_bias_grad: float32 [1024], replicated
- mlp_gain_grad: float32 [1024], replicated
- mlp_bias_grad: float32 [1024], replicated
- up_weight_grad: float32 [1024, 1024], P('pix', 'dp')
- up_bias_grad: float32 [1024], replicated
- down_weight_grad: float32 [1024, 1024], P('pix', 'dp')
- down_bias_grad: float32 [1024], replicated
- input_gain_grad: float32 [261], replicated
- input_bias_grad: float32 [261], replicated
Inputs may be any that keep to these rules, and one draw needn't show every extreme that they name: `image_sizes`: in every group one image is 112 x 112; the others have both sides between 16 and 32. `segment_ids`: A group's images fill its 16384 slots from the start, image 0 first, each taking height times width slots in a row; every later slot holds 4 and is padding. `coords`: row and column of the slot's pixel in its image, row-major along the image's slots; 0 and 0 in padding.
All inputs are finite; a program needn't handle non-finite values.
Results may differ from a plain program's by a relative error of at most 0.015.
Values may be sent and summed in bfloat16 or wider, within the bound.
A program may use at most 192 MiB of HBM per device.

v0:
```python
from functools import partial
import math

import jax
import jax.numpy as jnp
from jax import lax
from jax.sharding import PartitionSpec as P

BANDS = 64
MAXRES = 224


EPSILON = 1e-05


def layer_norm(inputs, norm_gain, norm_bias, along):
    centre = inputs - jnp.mean(inputs, axis=along, keepdims=True)
    spread = jnp.mean(centre * centre, axis=along, keepdims=True)
    scaled = centre * lax.rsqrt(spread + EPSILON)
    if along == 0:
        return scaled * norm_gain[:, None] + norm_bias[:, None]
    return scaled * norm_gain + norm_bias


def pixel_features(pixel_rgb, coords, segment_ids, image_sizes):
    image_count = image_sizes.shape[1]
    matches = segment_ids[None, :] == jnp.arange(image_count, dtype=jnp.int32)[:, None]
    row_span = jnp.sum(jnp.where(matches, image_sizes[0][:, None], 0), axis=0)
    col_span = jnp.sum(jnp.where(matches, image_sizes[1][:, None], 0), axis=0)
    pos_row = (
        2.0 * coords[0].astype(jnp.float32) / jnp.maximum(row_span - 1, 1).astype(jnp.float32) - 1.0
    )
    pos_col = (
        2.0 * coords[1].astype(jnp.float32) / jnp.maximum(col_span - 1, 1).astype(jnp.float32) - 1.0
    )
    band_index = jnp.arange(BANDS).astype(jnp.float32)
    frequency = 1.0 + band_index * (MAXRES / 2.0 - 1.0) / (BANDS - 1)

    def encode(position):
        phases = jnp.pi * frequency[:, None] * position[None, :]
        return jnp.concatenate([position[None, :], jnp.sin(phases), jnp.cos(phases)], axis=0)

    return jnp.concatenate(
        [pixel_rgb.astype(jnp.float32), encode(pos_row), encode(pos_col)], axis=0
    )


def shards(
    latents,
    pixel_rgb,
    coords,
    segment_ids,
    image_sizes,
    input_gain,
    input_bias,
    query_weight,
    query_bias,
    key_weight,
    value_weight,
    value_bias,
    out_weight,
    out_bias,
    latent_gain,
    latent_bias,
    mlp_gain,
    mlp_bias,
    up_weight,
    up_bias,
    down_weight,
    down_bias,
    cotangent,
):
    image_count = image_sizes.shape[1]
    scale_factor = 1.0 / math.sqrt(query_weight.shape[0])
    features = pixel_features(pixel_rgb, coords, segment_ids, image_sizes).astype(jnp.bfloat16)
    pixel_block = lax.all_to_all(features, "pix", split_axis=1, concat_axis=1, tiled=True)
    block_ids = lax.all_to_all(segment_ids, "pix", split_axis=0, concat_axis=0, tiled=True)
    member = block_ids[None, :] == jnp.arange(image_count, dtype=jnp.int32)[:, None]
    pixel_in_f, input_back = jax.vjp(
        partial(layer_norm, along=0), pixel_block.astype(jnp.float32), input_gain, input_bias
    )
    pixel_in = pixel_in_f.astype(jnp.bfloat16)
    key_rows = jnp.einsum(
        "ft,fd->td", pixel_in, key_weight, preferred_element_type=jnp.float32
    ).astype(jnp.bfloat16)
    value_rows = (
        jnp.einsum("ft,fd->td", pixel_in, value_weight, preferred_element_type=jnp.float32)
        + value_bias
    ).astype(jnp.bfloat16)
    latent_rows = latents.astype(jnp.float32)
    lat_in_f, latent_back = jax.vjp(
        partial(layer_norm, along=-1), latent_rows, latent_gain, latent_bias
    )
    lat_in = lat_in_f.astype(jnp.bfloat16)
    queries = (
        (jnp.dot(lat_in, query_weight, preferred_element_type=jnp.float32) + query_bias)
        * scale_factor
    ).astype(jnp.bfloat16)
    scores = jnp.einsum("ld,td->lt", queries, key_rows, preferred_element_type=jnp.float32)
    weights = jnp.where(member[:, None, :], jnp.exp(scores)[None], 0.0)
    weights_low = weights.astype(jnp.bfloat16)
    totals = jnp.sum(weights, axis=2)
    numerator = jnp.einsum(
        "nlt,td->nld", weights_low, value_rows, preferred_element_type=jnp.float32
    )
    summed_numerator, summed_totals = (
        lax.psum_scatter(numerator, "pix", scatter_dimension=0, tiled=True),
        lax.psum_scatter(totals, "pix", scatter_dimension=0, tiled=True),
    )
    own_numerator = summed_numerator[0]
    own_totals = summed_totals[0]
    attended = own_numerator / own_totals[:, None]
    attended_low = attended.astype(jnp.bfloat16)
    middle = (
        latent_rows
        + jnp.dot(attended_low, out_weight, preferred_element_type=jnp.float32)
        + out_bias
    )
    mid_in_f, mlp_back = jax.vjp(partial(layer_norm, along=-1), middle, mlp_gain, mlp_bias)
    mid_in = mid_in_f.astype(jnp.bfloat16)
    hidden = jnp.dot(mid_in, up_weight, preferred_element_type=jnp.float32) + up_bias
    active_f, gelu_back = jax.vjp(jax.nn.gelu, hidden)
    active = active_f.astype(jnp.bfloat16)
    latents_out = (
        middle + jnp.dot(active, down_weight, preferred_element_type=jnp.float32) + down_bias
    )[None]
    grad_out = cotangent[0]
    grad_down = grad_out.astype(jnp.bfloat16)
    down_grad = jnp.einsum("lf,ld->fd", active, grad_down, preferred_element_type=jnp.float32)
    down_bias_grad = jnp.sum(grad_down.astype(jnp.float32), axis=0)
    grad_active = jnp.einsum(
        "ld,fd->lf", grad_down, down_weight, preferred_element_type=jnp.float32
    )
    grad_hidden = gelu_back(grad_active)[0].astype(jnp.bfloat16)
    up_grad = jnp.einsum("ld,lf->df", mid_in, grad_hidden, preferred_element_type=jnp.float32)
    up_bias_grad = jnp.sum(grad_hidden.astype(jnp.float32), axis=0)
    grad_mid_in = jnp.einsum(
        "lf,df->ld", grad_hidden, up_weight, preferred_element_type=jnp.float32
    )
    grad_middle_norm, mlp_gain_grad, mlp_bias_grad = mlp_back(grad_mid_in)
    grad_middle = grad_out + grad_middle_norm
    grad_branch = grad_middle.astype(jnp.bfloat16)
    out_grad = jnp.einsum(
        "le,ld->ed", attended_low, grad_branch, preferred_element_type=jnp.float32
    )
    out_bias_grad = jnp.sum(grad_branch.astype(jnp.float32), axis=0)
    grad_attended = jnp.einsum(
        "ld,ed->le", grad_branch, out_weight, preferred_element_type=jnp.float32
    )
    grad_numerator = (grad_attended / own_totals[:, None]).astype(jnp.bfloat16)
    row_term = jnp.sum(grad_attended * attended, axis=1) / own_totals
    got_numerator, got_terms = (
        lax.all_gather(grad_numerator.astype(jnp.float32)[None], "pix", axis=0, tiled=True),
        lax.all_gather(row_term[None], "pix", axis=0, tiled=True),
    )
    numer_grads = got_numerator.astype(jnp.bfloat16)
    grad_weights = jnp.einsum(
        "nld,td->nlt", numer_grads, value_rows, preferred_element_type=jnp.float32
    )
    grad_scores = (weights * (grad_weights - got_terms[:, :, None])).astype(jnp.bfloat16)
    grad_values = jnp.einsum(
        "nlt,nld->td", weights_low, numer_grads, preferred_element_type=jnp.float32
    ).astype(jnp.bfloat16)
    summed_scores = jnp.sum(grad_scores.astype(jnp.float32), axis=0).astype(jnp.bfloat16)
    grad_keys = jnp.einsum(
        "lt,ld->td", summed_scores, queries, preferred_element_type=jnp.float32
    ).astype(jnp.bfloat16)
    query_part = jnp.einsum(
        "nlt,td->nld", grad_scores, key_rows, preferred_element_type=jnp.float32
    )
    grad_query_sum = lax.psum_scatter(query_part, "pix", scatter_dimension=0, tiled=True)[0]
    grad_queries = grad_query_sum.astype(jnp.bfloat16)
    key_grad = jnp.einsum("ft,td->fd", pixel_in, grad_keys, preferred_element_type=jnp.float32)
    value_grad = jnp.einsum("ft,td->fd", pixel_in, grad_values, preferred_element_type=jnp.float32)
    value_bias_grad = jnp.sum(grad_values.astype(jnp.float32), axis=0)
    grad_pixel_in = jnp.einsum(
        "td,fd->ft", grad_keys, key_weight, preferred_element_type=jnp.float32
    ) + jnp.einsum("td,fd->ft", grad_values, value_weight, preferred_element_type=jnp.float32)
    grad_features, input_gain_grad, input_bias_grad = input_back(grad_pixel_in)
    rgb_part = grad_features[:3].astype(jnp.bfloat16)
    rgb_grad = lax.all_to_all(rgb_part, "pix", split_axis=1, concat_axis=1, tiled=True)
    query_grad = (
        jnp.einsum("ld,le->de", lat_in, grad_queries, preferred_element_type=jnp.float32)
        * scale_factor
    )
    query_bias_grad = jnp.sum(grad_queries.astype(jnp.float32), axis=0) * scale_factor
    grad_lat_in = (
        jnp.einsum("le,de->ld", grad_queries, query_weight, preferred_element_type=jnp.float32)
        * scale_factor
    )
    grad_latent_norm, latent_gain_grad, latent_bias_grad = latent_back(grad_lat_in)
    latents_grad = grad_middle + grad_latent_norm
    first_sums = (
        lax.psum_scatter(latents_grad, "dp", scatter_dimension=1, tiled=True),
        lax.psum_scatter(query_grad, "dp", scatter_dimension=1, tiled=True),
        lax.psum_scatter(out_grad, "dp", scatter_dimension=1, tiled=True),
        lax.psum_scatter(up_grad, "dp", scatter_dimension=1, tiled=True),
        lax.psum_scatter(down_grad, "dp", scatter_dimension=1, tiled=True),
    )
    latent_part, query_piece, out_piece, up_piece, down_piece = first_sums
    final_sums = (
        lax.psum_scatter(latent_part, "pix", scatter_dimension=0, tiled=True),
        lax.psum_scatter(query_piece, "pix", scatter_dimension=0, tiled=True),
        lax.psum_scatter(out_piece, "pix", scatter_dimension=0, tiled=True),
        lax.psum_scatter(up_piece, "pix", scatter_dimension=0, tiled=True),
        lax.psum_scatter(down_piece, "pix", scatter_dimension=0, tiled=True),
    )
    latents_total, query_total, out_total, up_total, down_total = final_sums
    small_sums = lax.psum(
        (
            key_grad,
            value_grad,
            query_bias_grad,
            value_bias_grad,
            out_bias_grad,
            up_bias_grad,
            down_bias_grad,
            latent_gain_grad,
            latent_bias_grad,
            mlp_gain_grad,
            mlp_bias_grad,
            input_gain_grad,
            input_bias_grad,
        ),
        ("dp", "pix"),
    )
    (
        key_total,
        value_total,
        query_bias_total,
        value_bias_total,
        out_bias_total,
        up_bias_total,
        down_bias_total,
        latent_gain_total,
        latent_bias_total,
        mlp_gain_total,
        mlp_bias_total,
        input_gain_total,
        input_bias_total,
    ) = small_sums
    return (
        latents_out,
        rgb_grad,
        latents_total,
        query_total,
        query_bias_total,
        key_total,
        value_total,
        value_bias_total,
        out_total,
        out_bias_total,
        latent_gain_total,
        latent_bias_total,
        mlp_gain_total,
        mlp_bias_total,
        up_total,
        up_bias_total,
        down_total,
        down_bias_total,
        input_gain_total,
        input_bias_total,
    )


def solution(mesh):
    placed = (
        P(),
        P(None, ("dp", "pix")),
        P(None, ("dp", "pix")),
        P(("dp", "pix")),
        P(None, "dp"),
        P(),
        P(),
        P(),
        P(),
        P(),
        P(),
        P(),
        P(),
        P(),
        P(),
        P(),
        P(),
        P(),
        P(),
        P(),
        P(),
        P(),
        P(("dp", "pix"), None, None),
    )
    return jax.shard_map(
        shards,
        mesh=mesh,
        in_specs=placed,
        out_specs=(
            P(("dp", "pix"), None, None),
            P(None, ("dp", "pix")),
            P("pix", "dp"),
            P("pix", "dp"),
            P(),
            P(),
            P(),
            P(),
            P("pix", "dp"),
            P(),
            P(),
            P(),
            P(),
            P(),
            P("pix", "dp"),
            P(),
            P("pix", "dp"),
            P(),
            P(),
            P(),
        ),
        check_vma=False,
    )
```

profile of v0, /device:TPU:0, one launch (start us, length us, event | category | flops | bytes accessed | tf_op | source)
XLA Modules:
  0.0 1129.0 jit_solution(10489361129205184464)
XLA Ops:
  7.2 6.5 all-to-all-start
  17.5 8.5 fusion.35
  26.0 21.2 %concatenate.14 = bf16[261,4,1024]{2,0,1:T(8,128)(2,1)} concatenate(bf16[3,4,1024]{2,0,1:T(4,128)(2,1)S(1)} %bitcast.161, bf16[1,4,1024]{2,0,1:T(2,128)(2,1)S(1)} %bitcast.156, bf16[64,4,1024]{2,0,1:T(8,128)(2,1)} %get-tuple-element.68, bf16[64,4,1024]{2,0,1:T(8,128)(2,1)} %get-tuple-element.69, bf16[1,4,1024]{2,0,1:T(2,128)(2,1)S(1)} %bitcast.155, ...), dimensions={0} | concatenate | bytes 4276224 | tf_op jit(solution)/shard_map/concatenate | solution.py:43
  47.2 5.2 all-to-all-start.1
  56.6 45.0 %all-to-all-done.1 = bf16[261,4,1024]{2,0,1:T(8,128)(2,1)} async-done(((bf16[261,4,1024]{2,0,1:T(8,128)(2,1)}), bf16[261,4,1024]{2,0,1:T(8,128)(2,1)}, u32[]{:S(2)}, u32[]{:S(2)}) %all-to-all-start.1) | async-done | bytes 2138144 | tf_op jit(solution)/shard_map/all_to_all | solution.py:76
  105.9 3.3 copy.50
  110.2 3.9 copy.55
  117.2 5.0 convolution_convert_fusion.1
  122.3 6.8 fusion.9
  129.1 4.6 convolution_exponential_fusion
  133.7 3.2 copy-done.4
  136.9 21.8 %fusion.2 = f32[4,512,1024]{2,1,0:T(8,128)} fusion(bf16[4096,1024,1]{1,0,2:T(8,128)(2,1)} %fusion.9, f32[512,4096]{1,0:T(8,128)S(1)} %convolution_exponential_fusion, pred[4,4096]{1,0:T(4,128)(4,1)S(1)} %iota_compare_fusion.1), kind=kOutput, calls=%fused_computation.5 | convolution fusion | flops 17188257792 | bytes 25182208 | tf_op jit(solution)/shard_map/nlt,td->nld/dot_general | solution.py:103
  159.9 6.5 select_reduce_fusion
  166.4 10.9 all-reduce
  178.0 125.0 %reduce-scatter.13.cloned.1.call-done = f32[1,512,1024]{2,1,0:T(8,128)} async-done(((f32[4,512,1024]{2,1,0:T(8,128)}), f32[1,512,1024]{2,1,0:T(8,128)}) %reduce-scatter.13.cloned.1.call-update) | async-done | bytes 2097168 | tf_op jit(solution)/shard_map/reduce_scatter | solution.py:107
  303.0 3.6 fusion.73
  309.6 3.1 convert_reduce_fusion.4
  321.4 12.9 %all-gather.1 = f32[4,1,512]{2,1,0:T(1,128)S(1)} all-gather(f32[1,1,512]{2,1,0:T(1,128)S(1)} %divide_bitcast_fusion), channel_id=1, replica_groups=mesh['dp'=8,'pix'=4] {'pix'}, dimensions={0}, use_global_device_ids=true | all-gather | bytes 10240 | tf_op jit(solution)/shard_map/all_gather | solution.py:154
  334.3 68.0 %all-gather.4.cloned.1.call-done = bf16[2048,1024]{1,0:T(8,128)(2,1)} async-done(((bf16[512,1024]{1,0:T(8,128)(2,1)}), bf16[2048,1024]{1,0:T(8,128)(2,1)}) %all-gather.4.cloned.1.call-update) | async-done | bytes 4194320 | tf_op jit(solution)/shard_map/all_gather | solution.py:153
  402.4 29.2 %fusion.74 = (bf16[512,4096]{1,0:T(8,128)(2,1)}, bf16[4,512,4096]{2,1,0:T(8,128)(2,1)}) fusion(f32[4,512]{1,0:T(4,128)S(1)} %bitcast.162, bf16[4,512,1024]{2,1,0:T(8,128)(2,1)} %bitcast.167, bf16[4096,1024,1]{1,0,2:T(8,128)(2,1)} %fusion.9, f32[512,4096]{1,0:T(8,128)} %copy-done.4, pred[4,4096]{1,0:T(4,128)(4,1)S(1)} %iota_compare_fusion.1), kind=kOutput, calls=%fused_computation.145 | convolution fusion | flops 17219715072 | bytes 41967616 | tf_op jit(solution)/shard_map/nld,td->nlt/dot_general | solution.py:157
  431.6 24.0 %fusion.10 = f32[4,512,1024]{2,1,0:T(8,128)} fusion(bf16[4,512,4096]{2,1,0:T(8,128)(2,1)} %get-tuple-element.74, bf16[4096,1024]{1,0:T(8,128)(2,1)} %copy-done.59), kind=kOutput, calls=%fused_computation.16 | convolution fusion | flops 17179869184 | bytes 33554432 | tf_op jit(solution)/shard_map/nlt,td->nld/dot_general | solution.py:168
  455.6 5.9 fusion.52
  461.6 5.3 fusion.62
  467.1 5.2 fusion.40
  473.0 125.7 %reduce-scatter.15.cloned.1.call-done = f32[1,512,1024]{2,1,0:T(8,128)} async-done(((f32[4,512,1024]{2,1,0:T(8,128)}), f32[1,512,1024]{2,1,0:T(8,128)}) %reduce-scatter.15.cloned.1.call-update) | async-done | bytes 2097168 | tf_op jit(solution)/shard_map/reduce_scatter | solution.py:171
  598.7 3.8 multiply_reduce_fusion.6
  607.8 3.4 convolution_multiply_fusion
  611.3 42.7 %reduce-scatter.33.cloned.1.call-done = f32[1024,128]{1,0:T(8,128)} async-done(((f32[1024,1024]{1,0:T(8,128)}), f32[1024,128]{1,0:T(8,128)}) %reduce-scatter.33.cloned.1.call-update) | async-done | bytes 524304 | tf_op jit(solution)/shard_map/reduce_scatter | solution.py:198
  654.1 25.4 %convert_reduce_fusion = (f32[1024]{0:T(1024)S(1)}, bf16[4096,1024]{1,0:T(8,128)(2,1)}) fusion(bf16[4,512,1024]{2,1,0:T(8,128)(2,1)} %bitcast.168, f32[512,4096]{1,0:T(8,128)} %copy-done.4, pred[4,4096]{1,0:T(4,128)(4,1)S(1)} %iota_compare_fusion.1), kind=kOutput, calls=%fused_computation.7 | convolution fusion | flops 17200840704 | bytes 20992000 | tf_op jit(solution)/shard_map/nlt,nld->td/dot_general | solution.py:161
  679.4 29.5 %reduce-scatter.29.cloned.1.call-done = f32[1024,128]{1,0:T(8,128)} async-done(((f32[1024,1024]{1,0:T(8,128)}), f32[1024,128]{1,0:T(8,128)}) %reduce-scatter.29.cloned.1.call-update) | async-done | bytes 524304 | tf_op jit(solution)/shard_map/reduce_scatter | solution.py:197
  709.4 7.1 convolution_convert_fusion
  716.6 3.6 copy-done.56
  720.2 3.4 fusion.80
  723.5 39.9 %reduce-scatter.25.cloned.1.call-done = f32[1024,128]{1,0:T(8,128)} async-done(((f32[1024,1024]{1,0:T(8,128)}), f32[1024,128]{1,0:T(8,128)}) %reduce-scatter.25.cloned.1.call-update) | async-done | bytes 524304 | tf_op jit(solution)/shard_map/reduce_scatter | solution.py:196
  763.6 8.0 fusion.79
  771.5 7.2 fusion.81
  779.8 11.3 fusion.12
  791.0 17.4 %reduce-scatter.17.cloned.1.call-done = f32[512,128]{1,0:T(8,128)} async-done(((f32[512,1024]{1,0:T(8,128)}), f32[512,128]{1,0:T(8,128)}) %reduce-scatter.17.cloned.1.call-update) | async-done | bytes 262160 | tf_op jit(solution)/shard_map/reduce_scatter | solution.py:194
  808.7 7.0 fusion.67
  815.7 47.4 %reduce-scatter.21.cloned.1.call-done = f32[1024,128]{1,0:T(8,128)} async-done(((f32[1024,1024]{1,0:T(8,128)}), f32[1024,128]{1,0:T(8,128)}) %reduce-scatter.21.cloned.1.call-update) | async-done | bytes 524304 | tf_op jit(solution)/shard_map/reduce_scatter | solution.py:195
  864.7 4.6 all-to-all-start.2
  869.3 5.1 add_bitcast_fusion
  874.4 2.7 reduce_sum.333
  877.8 41.8 %all-reduce.1 = (f32[1024]{0:T(1024)}, f32[1024]{0:T(1024)}, f32[1024]{0:T(1024)}, f32[1024]{0:T(1024)}, f32[1024]{0:T(1024)}, /*index=5*/f32[1024]{0:T(1024)}, ...) all-reduce(f32[1024]{0:T(1024)S(1)} %broadcast_multiply_fusion.1, ...), channel_id=1, replica_groups=mesh['dp'=8,'pix'=4] {'dp','pix'}, use_global_device_ids=true, to_apply=%region_25.26 | all-reduce | flops 9738 | bytes 77904 | tf_op jit(solution)/shard_map/psum | solution.py:209
  919.6 14.1 %reduce-scatter.27.cloned.1.call-done = f32[256,128]{1,0:T(8,128)} async-done(((f32[1024,128]{1,0:T(8,128)}), f32[256,128]{1,0:T(8,128)}) %reduce-scatter.27.cloned.1.call-update) | async-done | bytes 131088 | tf_op jit(solution)/shard_map/reduce_scatter | solution.py:204
  933.7 140.1 %all-reduce.5.cloned.1.call-done = (f32[261,1024]{1,0:T(8,128)}, f32[261,1024]{1,0:T(8,128)}) async-done(((f32[261,1024]{1,0:T(8,128)}, f32[261,1024]{1,0:T(8,128)}), (f32[261,1024]{1,0:T(8,128)}, f32[261,1024]{1,0:T(8,128)})) %all-reduce.5.cloned.1.call-update) | async-done | bytes 2138128 | tf_op jit(solution)/shard_map/psum | solution.py:209
  1073.9 21.8 %reduce-scatter.19.cloned.1.call-done = f32[128,128]{1,0:T(8,128)} async-done(((f32[512,128]{1,0:T(8,128)}), f32[128,128]{1,0:T(8,128)}) %reduce-scatter.19.cloned.1.call-update) | async-done | bytes 65552 | tf_op jit(solution)/shard_map/reduce_scatter | solution.py:202
  1095.6 22.7 %reduce-scatter.23.cloned.1.call-done = f32[256,128]{1,0:T(8,128)} async-done(((f32[1024,128]{1,0:T(8,128)}), f32[256,128]{1,0:T(8,128)}) %reduce-scatter.23.cloned.1.call-update) | async-done | bytes 131088 | tf_op jit(solution)/shard_map/reduce_scatter | solution.py:203
  (203 shorter events, 44.3 us)
Async XLA Ops:
  7.2 299.8 %copy-start = (bf16[1024,1024]{1,0:T(8,128)(2,1)S(1)}, bf16[1024,1024]{1,0:T(8,128)(2,1)}, u32[]{:S(2)}) copy-start(bf16[1024,1024]{1,0:T(8,128)(2,1)} %param.41) | copy-start | bytes 6291460
  7.2 18.8 %copy-start.24 = (bf16[3,4096]{1,0:T(4,128)(2,1)S(1)}, bf16[3,4096]{1,0:T(4,128)(2,1)}, u32[]{:S(2)}) copy-start(bf16[3,4096]{1,0:T(4,128)(2,1)} %param.24) | copy-start | bytes 73732
  7.2 40.0 %all-to-all-start = ((s32[4,1024,1]{1,2,0:T(1,128)}), s32[4,1024,1]{1,2,0:T(1,128)S(1)}, u32[]{:S(2)}, u32[]{:S(2)}) async-start(s32[4,1024,1]{1,2,0:T(1,128)} %bitcast.157), calls=%async_computation | async-start | bytes 32768 | tf_op jit(solution)/shard_map/all_to_all | solution.py:77
  47.2 5.5 copy-start.3
  47.2 54.4 %all-to-all-start.1 = ((bf16[261,4,1024]{2,0,1:T(8,128)(2,1)}), bf16[261,4,1024]{2,0,1:T(8,128)(2,1)}, u32[]{:S(2)}, u32[]{:S(2)}) async-start(bf16[261,4,1024]{2,0,1:T(8,128)(2,1)} %concatenate.14), calls=%async_computation.1 | async-start | bytes 4325376 | tf_op jit(solution)/shard_map/all_to_all | solution.py:76
  52.4 250.5 %reduce-scatter.13.cloned.1.call-start = ((), (), s32[]{:S(2)}) async-start(), calls=%async_computation.15 | async-start | bytes 10485760 | tf_op jit(solution)/shard_map/reduce_scatter | solution.py:107
  52.9 3.7 copy-start.27
  53.3 3.3 copy-start.29
  103.6 10.6 copy-start.18
  105.8 3.3 copy-start.22
  105.9 8.3 copy-start.20
  110.2 5.9 copy-start.25
  110.2 5.9 copy-start.40
  117.2 5.0 copy-start.9
  117.2 5.0 copy-start.16
  117.2 5.1 copy-start.48
  122.3 6.8 copy-start.59
  122.3 6.8 copy-start.60
  158.7 243.6 %all-gather.4.cloned.1.call-start = ((), (), s32[]{:S(2)}) async-start(), calls=%async_computation.27 | async-start | bytes 5242880 | tf_op jit(solution)/shard_map/all_gather | solution.py:153
  159.9 143.0 %copy-start.49 = (f32[1024]{0:T(1024)S(1)}, f32[1024]{0:T(1024)}, u32[]{:S(2)}) copy-start(f32[1024]{0:T(1024)} %param.36) | copy-start | bytes 12292
  306.6 8.4 copy-start.5
  316.7 4.0 copy-start.15
  320.7 278.0 %reduce-scatter.15.cloned.1.call-start = ((), (), s32[]{:S(2)}) async-start(), calls=%async_computation.16 | async-start | bytes 10485760 | tf_op jit(solution)/shard_map/reduce_scatter | solution.py:171
  455.6 198.4 %reduce-scatter.33.cloned.1.call-start = ((), (), s32[]{:S(2)}) async-start(), calls=%async_computation.25 | async-start | bytes 4718592 | tf_op jit(solution)/shard_map/reduce_scatter | solution.py:198
  461.5 247.4 %reduce-scatter.29.cloned.1.call-start = ((), (), s32[]{:S(2)}) async-start(), calls=%async_computation.23 | async-start | bytes 4718592 | tf_op jit(solution)/shard_map/reduce_scatter | solution.py:197
  466.9 296.6 %reduce-scatter.25.cloned.1.call-start = ((), (), s32[]{:S(2)}) async-start(), calls=%async_computation.21 | async-start | bytes 4718592 | tf_op jit(solution)/shard_map/reduce_scatter | solution.py:196
  472.3 126.4 %copy-start.28 = (f32[512]{0:T(512)S(1)}, f32[512]{0:T(512)}, u32[]{:S(2)}) copy-start(f32[512]{0:T(512)} %copy-done.27) | copy-start | bytes 6148
  472.3 336.1 %reduce-scatter.17.cloned.1.call-start = ((), (), s32[]{:S(2)}) async-start(), calls=%async_computation.17 | async-start | bytes 2359296 | tf_op jit(solution)/shard_map/reduce_scatter | solution.py:194
  473.0 129.5 %copy-start.30 = (f32[512]{0:T(512)S(1)}, f32[512]{0:T(512)}, u32[]{:S(2)}) copy-start(f32[512]{0:T(512)} %copy-done.29) | copy-start | bytes 6148
  473.0 129.5 %copy-start.32 = (f32[512]{0:T(512)S(1)}, f32[512]{0:T(512)}, u32[]{:S(2)}) copy-start(f32[512]{0:T(512)} %copy-done.31) | copy-start | bytes 6148
  606.2 256.9 %reduce-scatter.21.cloned.1.call-start = ((), (), s32[]{:S(2)}) async-start(), calls=%async_computation.19 | async-start | bytes 4718592 | tf_op jit(solution)/shard_map/reduce_scatter | solution.py:195
  611.3 308.4 %reduce-scatter.35.cloned.1.call-start = ((), (), s32[]{:S(2)}) async-start(), calls=%async_computation.26 | async-start | bytes 655360 | tf_op jit(solution)/shard_map/reduce_scatter | solution.py:206
  654.0 55.4 %copy-start.61 = (bf16[512,1024]{1,0:T(8,128)(2,1)S(1)}, bf16[512,1024]{1,0:T(8,128)(2,1)}, u32[]{:S(2)}) copy-start(bf16[512,1024]{1,0:T(8,128)(2,1)} %multiply_convert_fusion.1) | copy-start | bytes 3145732
  654.0 265.6 %reduce-scatter.31.cloned.1.call-start = ((), (), s32[]{:S(2)}) async-start(), calls=%async_computation.24 | async-start | bytes 655360 | tf_op jit(solution)/shard_map/reduce_scatter | solution.py:205
  709.0 224.8 %reduce-scatter.27.cloned.1.call-start = ((), (), s32[]{:S(2)}) async-start(), calls=%async_computation.22 | async-start | bytes 655360 | tf_op jit(solution)/shard_map/reduce_scatter | solution.py:204
  709.4 10.7 copy-start.10
  716.6 3.6 copy-start.56
  720.2 43.4 %copy-start.46 = (bf16[261,1024]{1,0:T(8,128)(2,1)S(1)}, bf16[261,1024]{1,0:T(8,128)(2,1)}, u32[]{:S(2)}) copy-start(bf16[261,1024]{1,0:T(8,128)(2,1)} %param.32) | copy-start | bytes 1603588
  763.5 310.4 %all-reduce.5.cloned.1.call-start = ((), (), s32[]{:S(2)}) async-start(), calls=%async_computation.28 | async-start | bytes 4325376 | tf_op jit(solution)/shard_map/psum | solution.py:209
  763.5 8.0 copy-start.11
  778.7 12.3 %copy-start.23 = (f32[1,8,4,128]{3,2,1,0:T(4,128)S(1)}, f32[1,8,4,128]{3,2,1,0:T(4,128)}, u32[]{:S(2)}) copy-start(f32[1,8,4,128]{3,2,1,0:T(4,128)} %copy-done.22) | copy-start | bytes 49156
  778.7 316.9 %reduce-scatter.19.cloned.1.call-start = ((), (), s32[]{:S(2)}) async-start(), calls=%async_computation.18 | async-start | bytes 327680 | tf_op jit(solution)/shard_map/reduce_scatter | solution.py:202
  808.4 309.9 %reduce-scatter.23.cloned.1.call-start = ((), (), s32[]{:S(2)}) async-start(), calls=%async_computation.20 | async-start | bytes 655360 | tf_op jit(solution)/shard_map/reduce_scatter | solution.py:203
  808.7 60.6 %copy-start.6 = (f32[512,1024]{1,0:T(8,128)S(1)}, f32[512,1024]{1,0:T(8,128)}, u32[]{:S(2)}) copy-start(f32[512,1024]{1,0:T(8,128)} %copy-done.5) | copy-start | bytes 6291460
  808.7 60.6 %copy-start.53 = (f32[1024]{0:T(1024)S(1)}, f32[1024]{0:T(1024)}, u32[]{:S(2)}) copy-start(f32[1024]{0:T(1024)} %param.44) | copy-start | bytes 12292
  864.7 12.4 %all-to-all-start.2 = ((bf16[3,4,1024]{2,0,1:T(4,128)(2,1)}), bf16[3,4,1024]{2,0,1:T(4,128)(2,1)S(1)}, u32[]{:S(2)}, u32[]{:S(2)}) async-start(bf16[3,4,1024]{2,0,1:T(4,128)(2,1)} %bitcast.19), calls=%async_computation.3 | async-start | bytes 65536 | tf_op jit(solution)/shard_map/all_to_all | solution.py:181
  1073.9 47.5 %copy-start.14 = (f32[261,1024]{1,0:T(8,128)S(1)}, f32[261,1024]{1,0:T(8,128)}, u32[]{:S(2)}) copy-start(f32[261,1024]{1,0:T(8,128)} %get-tuple-element.113) | copy-start | bytes 3207172
  1118.3 4.0 copy-start.1
  (31 other events, 46.3 us)
Sparse Core Ops, SparseCore 0:
  158.8 144.0 reduce-scatter.12
  320.8 81.4 all-gather.3
  455.7 142.9 reduce-scatter.14
  601.9 52.0 reduce-scatter.32
  657.6 51.3 reduce-scatter.28
  712.1 51.2 reduce-scatter.24
  767.1 41.2 reduce-scatter.16
  811.8 51.2 reduce-scatter.20
  866.1 21.6 reduce-scatter.34
  890.5 20.0 reduce-scatter.30
  913.6 20.1 reduce-scatter.26
  940.9 132.9 all-reduce.4
  1076.7 18.9 reduce-scatter.18
  1098.4 19.8 reduce-scatter.22
where the time goes:
time: 1130 us
  waiting for transfers between devices  739 us (65%)
  matrix products  197 us (17%)
  blocking collectives  65.6 us (6%)
  local copies, waits for them, and re-layouts  53.4 us (5%)
  other arithmetic  40.7 us (4%)
  starting transfers between devices  17.8 us (2%)
  between operations  14.7 us (1%)
    psum x1, waiting for transfers between devices, shards(): lax.psum((key_grad, value_grad, query_bias_grad, value_bias_grad, out_bia...  140 us
    reduce_scatter x1, waiting for transfers between devices, shards(): lax.psum_scatter(query_part, 'pix', scatter_dimension=0, tiled=True)[0]  126 us
    reduce_scatter x1, waiting for transfers between devices, shards(): lax.psum_scatter(numerator, 'pix', scatter_dimension=0, tiled=True)  125 us
    all_gather x1, waiting for transfers between devices, shards(): lax.all_gather(grad_numerator.astype(jnp.float32)[None], 'pix', axis=0, t...  68 us
    reduce_scatter x1, waiting for transfers between devices, shards(): lax.psum_scatter(query_grad, 'dp', scatter_dimension=1, tiled=True)  47.4 us
    all_to_all x1, waiting for transfers between devices, shards(): lax.all_to_all(features, 'pix', split_axis=1, concat_axis=1, tiled=True)  45 us
    reduce_scatter x1, waiting for transfers between devices, shards(): lax.psum_scatter(down_grad, 'dp', scatter_dimension=1, tiled=True)  42.7 us
    psum x1, blocking collectives, shards(): lax.psum((key_grad, value_grad, query_bias_grad, value_bias_grad, out_bia...  41.8 us
  transfers between devices with their start and end apart: 17, of which 13 were waited for; matrix products, arithmetic and copies ran while one was open for 13% of the time, Pallas kernels for 0%

commit v1 on v0

v1 whole, which is shorter than its diff:
```python
from functools import partial
import math

import jax
import jax.numpy as jnp
from jax import lax
from jax.sharding import PartitionSpec as P

BANDS = 64
MAXRES = 224
EPSILON = 1e-05
FEAT = 4 * BANDS + 5
WIDE = FEAT + 3

bf16 = jnp.bfloat16
f32 = jnp.float32


def dot(a, b, dims):
    return lax.dot_general(a, b, (dims, ((), ())), preferred_element_type=f32)


def nn(a, b):
    return dot(a, b, ((1,), (0,)))


def nt(a, b):
    return dot(a, b, ((1,), (1,)))


def tn(a, b):
    return dot(a, b, ((0,), (0,)))


def reorder(rows):
    b = 2 * BANDS
    pad = [(0, WIDE - FEAT)] + [(0, 0)] * (rows.ndim - 1)
    return jnp.pad(
        jnp.concatenate([rows[4 : 4 + b], rows[5 + b :], rows[0:4], rows[4 + b : 5 + b]], axis=0), pad
    )


def restore(rows):
    b = 2 * BANDS
    return jnp.concatenate(
        [rows[2 * b : 2 * b + 4], rows[:b], rows[2 * b + 4 : 2 * b + 5], rows[b : 2 * b]], axis=0
    )


def centred(rows, axis):
    live = (lax.broadcasted_iota(jnp.int32, rows.shape, axis) < FEAT).astype(f32)
    return (rows - jnp.sum(rows, axis=axis, keepdims=True) * (1.0 / FEAT)) * live


def layout(sizes, slots):
    images = sizes.shape[1]
    slot = jnp.arange(slots, dtype=jnp.int32)
    segment = jnp.zeros((slots,), jnp.int32)
    start = jnp.zeros((slots,), jnp.int32)
    end = jnp.int32(0)
    for i in range(images):
        end = end + sizes[0, i] * sizes[1, i]
        past = slot >= end
        segment = segment + past.astype(jnp.int32)
        start = jnp.where(past, end, start)
    high = jnp.zeros((slots,), jnp.int32)
    wide = jnp.zeros((slots,), jnp.int32)
    for i in range(images):
        high = jnp.where(segment == i, sizes[0, i], high)
        wide = jnp.where(segment == i, sizes[1, i], wide)
    local = jnp.where(segment < images, slot - start, 0)
    row = local // jnp.maximum(wide, 1)
    col = local - row * wide
    y = 2.0 * row.astype(f32) / jnp.maximum(high - 1, 1).astype(f32) - 1.0
    x = 2.0 * col.astype(f32) / jnp.maximum(wide - 1, 1).astype(f32) - 1.0
    return segment, y, x


def pixel_features(rgb, y, x):
    frequency = 1.0 + jnp.arange(BANDS).astype(f32) * ((MAXRES / 2.0 - 1.0) / (BANDS - 1))
    py = jnp.pi * frequency[:, None] * y[None]
    px = jnp.pi * frequency[:, None] * x[None]
    rest = jnp.concatenate(
        [rgb.astype(f32), y[None], x[None], jnp.zeros((WIDE - FEAT, y.shape[0]), f32)], axis=0
    )
    return jnp.concatenate(
        [jnp.sin(py), jnp.cos(py), jnp.sin(px), jnp.cos(px), rest], axis=0
    ).astype(bf16)


def norm(rows):
    centre = rows - jnp.mean(rows, axis=-1, keepdims=True)
    scale = lax.rsqrt(jnp.mean(centre * centre, axis=-1, keepdims=True) + EPSILON)
    return centre * scale, scale


def norm_back(grad, unit, scale):
    return (
        grad
        - jnp.mean(grad, axis=-1, keepdims=True)
        - unit * jnp.mean(grad * unit, axis=-1, keepdims=True)
    ) * scale


def shards(
    latents,
    pixel_rgb,
    coords,
    segment_ids,
    image_sizes,
    input_gain,
    input_bias,
    query_weight,
    query_bias,
    key_weight,
    value_weight,
    value_bias,
    out_weight,
    out_bias,
    latent_gain,
    latent_bias,
    mlp_gain,
    mlp_bias,
    up_weight,
    up_bias,
    down_weight,
    down_bias,
    cotangent,
):
    images = image_sizes.shape[1]
    count, width = latents.shape
    parts = lax.axis_size("pix")
    place = lax.axis_index("pix")
    own = count // parts
    factor = 1.0 / math.sqrt(query_weight.shape[0])
    slots = pixel_rgb.shape[1] * parts

    rgb = lax.all_gather(pixel_rgb, "pix", axis=1, tiled=True)
    cot_low = cotangent[0].astype(bf16).reshape(parts, own, width)
    cot = lax.all_to_all(cot_low, "pix", split_axis=0, concat_axis=0, tiled=True).astype(f32)

    gain = reorder(input_gain)
    bias = reorder(input_bias)
    wk = reorder(key_weight)
    wv = reorder(value_weight)

    latent_rows = latents.astype(f32)
    lat_unit, lat_scale = norm(latent_rows)
    lat_in = (lat_unit * latent_gain + latent_bias).astype(bf16)
    queries = ((nn(lat_in, query_weight) + query_bias) * factor).astype(bf16)
    own_queries = lax.dynamic_slice_in_dim(queries, place * own, own, axis=0)
    own_latents = lax.dynamic_slice_in_dim(latent_rows, place * own, own, axis=0)

    qk = nt(own_queries, wk)
    qc = centred(qk * gain, 1).astype(bf16)
    qb = jnp.sum(qk * bias, axis=1)
    segment, y, x = layout(image_sizes, slots)
    feat = pixel_features(rgb, y, x)
    featf = feat.astype(f32)
    mean = jnp.sum(featf, axis=0) * (1.0 / FEAT)
    spread = jnp.sum(featf * featf, axis=0) * (1.0 / FEAT) - mean * mean
    scale = lax.rsqrt(spread + EPSILON)
    raw = nn(qc, feat) * scale
    member = (segment[None] == jnp.arange(images)[:, None]).astype(f32)
    weights = jnp.where(segment < images, jnp.exp(raw + qb[:, None]), 0.0)
    totals = dot(member, weights, ((1,), (1,)))
    scaled = ((weights * scale)[None] * member[:, None]).astype(bf16).reshape(images * own, slots)
    mix = centred(nt(scaled, feat), 1)
    unit = mix / totals.reshape(-1, 1)
    px = (unit * gain + bias).astype(bf16)

    wvo = nn(wv, out_weight).astype(bf16)
    const = nn(value_bias[None].astype(f32), out_weight.astype(f32))[0] + out_bias
    middle = jnp.tile(own_latents, (images, 1)) + nn(px, wvo) + const
    mid_unit, mid_scale = norm(middle)
    mid_in = (mid_unit * mlp_gain + mlp_bias).astype(bf16)
    hidden = nn(mid_in, up_weight) + up_bias
    k = math.sqrt(2.0 / math.pi)
    th = jnp.tanh(k * (hidden + 0.044715 * hidden**3))
    active = (0.5 * hidden * (1.0 + th)).astype(bf16)
    slope = 0.5 * (1.0 + th) + 0.5 * hidden * (1.0 - th * th) * k * (1.0 + 3 * 0.044715 * hidden**2)
    out = (middle + nn(active, down_weight) + down_bias).astype(bf16).reshape(images, own, width)
    latents_out = (
        lax.all_to_all(out, "pix", split_axis=0, concat_axis=0, tiled=True)
        .reshape(1, count, width)
        .astype(f32)
    )
    cot = cot.reshape(images * own, width)
    grad_down = cot.astype(bf16)
    down_grad = tn(active, grad_down)
    down_bias_grad = jnp.sum(cot, axis=0)
    grad_hidden = (slope * nt(grad_down, down_weight)).astype(bf16)
    up_grad = tn(mid_in, grad_hidden)
    up_bias_grad = jnp.sum(grad_hidden.astype(f32), axis=0)
    grad_mid = nt(grad_hidden, up_weight)
    mlp_gain_grad = jnp.sum(grad_mid * mid_unit, axis=0)
    mlp_bias_grad = jnp.sum(grad_mid, axis=0)
    grad_middle = cot + norm_back(grad_mid * mlp_gain, mid_unit, mid_scale)
    branch = grad_middle.astype(bf16)
    moment = tn(px, branch)
    out_bias_grad = jnp.sum(branch.astype(f32), axis=0)
    latents_part = jnp.sum(grad_middle.reshape(images, own, width), axis=0)

    gx = nt(branch, wvo)
    gain_part = jnp.sum(gx * unit, axis=0)
    bias_part = jnp.sum(gx, axis=0)
    gc = centred(gx / totals.reshape(-1, 1) * gain, 1).astype(bf16)
    level = jnp.sum(gc.astype(f32) * unit, axis=1).reshape(images, own)

    pull = nn(gc, feat).reshape(images, own, slots)
    pull = jnp.sum(pull * member[:, None], axis=0) * scale
    level_t = dot(level, member, ((0,), (0,)))
    gs = weights * (pull - level_t)
    gs_sum = jnp.sum(gs, axis=1)
    dq = centred(nt((gs * scale).astype(bf16), feat), 1)
    lean = jnp.sum(gs * raw + weights * pull, axis=0) * (1.0 / FEAT)
    ext = slice(4 * BANDS, 4 * BANDS + 3)
    grad_ext = tn(qc[:, ext], gs.astype(bf16))
    back = tn(gc[:, ext].reshape(images, own, 3)[0] * 0, gs.astype(bf16))
    for n in range(images):
        back = back + member[n] * tn(gc[n * own : (n + 1) * own, ext], weights.astype(bf16))
    u_ext = (featf[ext] - mean) * scale
    rgb_part = (grad_ext + back - u_ext * lean) * scale
    rgb_grad = lax.psum_scatter(rgb_part, "pix", scatter_dimension=1, tiled=True).astype(bf16)

    latents_sum = lax.psum_scatter(latents_part, "dp", scatter_dimension=1, tiled=True)
    down_total = lax.psum_scatter(
        lax.psum_scatter(down_grad, "dp", scatter_dimension=1, tiled=True),
        "pix", scatter_dimension=0, tiled=True)
    up_total = lax.psum_scatter(
        lax.psum_scatter(up_grad, "dp", scatter_dimension=1, tiled=True),
        "pix", scatter_dimension=0, tiled=True)
    moment_t, ob, ub, db, mg, mb, gp, bp = lax.psum(
        (moment, out_bias_grad, up_bias_grad, down_bias_grad, mlp_gain_grad, mlp_bias_grad, gain_part, bias_part),
        ("dp", "pix"))
    dq_all = lax.psum(jnp.concatenate([dq, gs_sum[:, None]], axis=1), "dp")
    dq_all = lax.all_gather(dq_all, "pix", axis=0, tiled=True)
    dq_t, gs_t = dq_all[:, :WIDE], dq_all[:, WIDE]

    group = lax.axis_index("dp")
    groups = lax.axis_size("dp")
    cols = width // groups
    rows = width // parts
    moment_low = moment_t.astype(bf16)
    my_wv = lax.dynamic_slice_in_dim(wv, place * rows, rows, axis=1)
    my_vb = lax.dynamic_slice_in_dim(value_bias, place * rows, rows, axis=0)
    out_total = tn(my_wv, lax.dynamic_slice_in_dim(moment_low, group * cols, cols, axis=1)) + (
        my_vb[:, None] * lax.dynamic_slice_in_dim(ob, group * cols, cols, axis=0)[None]
    )
    value_total = restore(nt(moment_low, out_weight))
    value_bias_total = nt(ob[None], out_weight.astype(f32))[0]
    qk_all = nt(queries, wk)
    dx = dq_t * gain + gs_t[:, None] * bias
    gain_t = restore(gp + jnp.sum(qk_all * dq_t, axis=0))
    bias_t = restore(bp + jnp.sum(qk_all * gs_t[:, None], axis=0))
    dx_low = dx.astype(bf16)
    key_total = restore(tn(dx_low, queries))
    gq = nn(dx_low, wk) * factor
    gq_low = gq.astype(bf16)
    query_bias_total = jnp.sum(gq, axis=0)
    query_total = tn(
        lax.dynamic_slice_in_dim(lat_in, place * rows, rows, axis=1),
        lax.dynamic_slice_in_dim(gq_low, group * cols, cols, axis=1),
    )
    grad_lat = nt(gq_low, query_weight)
    latent_gain_total = jnp.sum(grad_lat * lat_unit, axis=0)
    latent_bias_total = jnp.sum(grad_lat, axis=0)
    lat_back = norm_back(grad_lat * latent_gain, lat_unit, lat_scale)
    latents_total = latents_sum + lax.dynamic_slice(
        lat_back, (place * own, group * cols), (own, cols)
    )
    return (
        latents_out,
        rgb_grad,
        latents_total,
        query_total,
        query_bias_total,
        key_total,
        value_total,
        value_bias_total,
        out_total,
        ob,
        latent_gain_total,
        latent_bias_total,
        mg,
        mb,
        up_total,
        ub,
        down_total,
        db,
        gain_t,
        bias_t,
    )


def solution(mesh):
    whole = P()
    placed = (
        whole,
        P(None, ("dp", "pix")),
        P(None, ("dp", "pix")),
        P(("dp", "pix")),
        P(None, "dp"),
    ) + (whole,) * 17 + (P(("dp", "pix"), None, None),)
    square = P("pix", "dp")
    return jax.shard_map(
        shards,
        mesh=mesh,
        in_specs=placed,
        out_specs=(
            P(("dp", "pix"), None, None),
            P(None, ("dp", "pix")),
            square,
            square,
            whole,
            whole,
            whole,
            whole,
            square,
            whole,
            whole,
            whole,
            whole,
            whole,
            square,
            whole,
            square,
            whole,
            whole,
            whole,
        ),
        check_vma=False,
    )
```

time: 1130 us -> 672 us (0.59)
  waiting for transfers between devices: 739 us -> 229 us
  other arithmetic: 40.7 us -> 130 us
  matrix products: 197 us -> 120 us
  blocking collectives: 65.6 us -> 86.6 us
  local copies, waits for them, and re-layouts: 53.4 us -> 65.5 us
    reduce_scatter x10 -> x3, waiting for transfers between devices: 414 us -> 80.7 us  [the longest x1 34.9 us: shards(): lax.psum_scatter(latents_part, 'dp', scatter_dimension=1, tiled=True)]
    unnamed x14 -> x8, waiting for transfers between devices: 0.23 us -> 141 us
    psum x1, waiting for transfers between devices: 140 us -> 0.01 us  [shards(): dq_all = lax.psum(jnp.concatenate([dq, gs_sum[:, None]], axis=1), 'dp')]
    dot_general x24 -> x33, matrix products: 197 us -> 120 us  [dot(): return lax.dot_general(a, b, (dims, ((), ())), preferred_element_type=f32)]
    all_gather x1 -> x0, waiting for transfers between devices: 68 us -> none  [shards(): lax.all_gather(grad_numerator.astype(jnp.float32)[None], 'pix', axis=0, t...]
    all_to_all x3 -> x2, waiting for transfers between devices: 45 us -> 0.01 us  [the longest x1 0.01 us: shards(): lax.all_to_all(out, 'pix', split_axis=0, concat_axis=0, tiled=True)]
    reduce_scatter x1, waiting for transfers between devices: 42.7 us -> 6.92 us  [shards(): lax.psum_scatter(down_grad, 'dp', scatter_dimension=1, tiled=True)]
    another operation x2, other arithmetic: 10 us -> 44.1 us
  transfers between devices with their start and end apart: 17 -> 9, of which waited for: 13 -> 5; matrix products, arithmetic and copies ran while one was open for 13% -> 37% of each run, Pallas kernels for 0% -> 0%
where the time goes in v1:
time: 672 us; the launch traced here: 663 us
  waiting for transfers between devices  229 us (34%)
  other arithmetic  130 us (19%)
  matrix products  120 us (18%)
  blocking collectives  86.6 us (13%)
  local copies, waits for them, and re-layouts  65.5 us (10%)
  between operations  20.6 us (3%)
  starting transfers between devices  11.4 us (2%)
    unnamed x8, waiting for transfers between devices  141 us
    dot_general x33, matrix products, dot(): return lax.dot_general(a, b, (dims, ((), ())), preferred_element_type=f32)  120 us
    psum x1, blocking collectives, shards(): lax.psum((moment, out_bias_grad, up_bias_grad, down_bias_grad, mlp_gain_g...  56.1 us
    another operation x2, other arithmetic  44.1 us
    concatenate x1, local copies, waits for them, and re-layouts, pixel_features(): jnp.concatenate([jnp.sin(py), jnp.cos(py), jnp.sin(px), jnp.cos(px), rest...  39.5 us
    reduce_scatter x1, waiting for transfers between devices, shards(): lax.psum_scatter(latents_part, 'dp', scatter_dimension=1, tiled=True)  34.9 us
    reduce_scatter x1, waiting for transfers between devices, shards(): lax.psum_scatter(lax.psum_scatter(down_grad, 'dp', scatter_dimension=1, t...  22.9 us
    reduce_scatter x1, waiting for transfers between devices, shards(): lax.psum_scatter(lax.psum_scatter(up_grad, 'dp', scatter_dimension=1, til...  22.8 us
  transfers between devices with their start and end apart: 9, of which 5 were waited for; matrix products, arithmetic and copies ran while one was open for 37% of the time, Pallas kernels for 0%

profile of v1, /device:TPU:0, one launch (start us, length us, event | category | flops | bytes accessed | tf_op | source)
XLA Modules:
  0.0 662.8 jit_solution(16492756846132314575)
XLA Ops:
  7.2 2.9 convert_element_type.305
  10.1 6.4 all-to-all-start.1
  22.4 6.0 divide_add_fusion
  28.4 12.1 %add_convert_fusion.5 = (bf16[1,16384]{1,0:T(2,128)(2,1)}, bf16[1,16384]{1,0:T(2,128)(2,1)}) fusion(s32[]{:T(128)S(6)} %add.341, s32[]{:T(128)S(6)} %add.339, s32[]{:T(128)S(6)} %add.337, s32[]{:T(128)S(6)} %mul.532, s32[]{:T(128)} %bitcast.2, s32[]{:T(128)} %bitcast.4, s32[]{:T(128)} %bitcast.6, s32[]{:T(128)} %bitcast.8, s32[]{:T(128)} %bitcast.1, ...), kind=kLoop, calls=%fused_computation.159 | loop fusion | flops 950272 | bytes 65584 | tf_op jit(solution)/shard_map/convert.7
  41.8 2.0 fusion.107
  48.1 14.1 %all_gather.6 = bf16[3,16384]{1,0:T(4,128)(2,1)S(1)} all-gather(bf16[3,4096]{1,0:T(4,128)(2,1)S(1)} %copy-done.38), channel_id=1, replica_groups=mesh['dp'=8,'pix'=4] {'pix'}, dimensions={1}, use_global_device_ids=true | all-gather | bytes 122880 | tf_op jit(solution)/shard_map/all_gather | solution.py:138
  62.3 32.1 %fusion.14 = (bf16[64,16384]{1,0:T(8,128)(2,1)}, bf16[64,16384]{1,0:T(8,128)(2,1)}, bf16[64,16384]{1,0:T(8,128)(2,1)}, bf16[64,16384]{1,0:T(8,128)(2,1)}) fusion(f32[16384]{0:T(1024)S(1)} %get-tuple-element.113, f32[64]{0:T(128)S(1)} %add_multiply_fusion, f32[16384]{0:T(1024)S(1)} %get-tuple-element.114), kind=kLoop, calls=%fused_computation.31 | loop fusion | flops 6291456 | bytes 8519936 | tf_op jit(solution)/shard_map/convert.4
  94.4 39.5 %concatenate.33 = bf16[264,16384]{1,0:T(8,128)(2,1)} concatenate(bf16[64,16384]{1,0:T(8,128)(2,1)} %get-tuple-element.92, bf16[64,16384]{1,0:T(8,128)(2,1)} %get-tuple-element.93, bf16[64,16384]{1,0:T(8,128)(2,1)} %get-tuple-element.71, bf16[64,16384]{1,0:T(8,128)(2,1)} %get-tuple-element.70, bf16[3,16384]{1,0:T(4,128)(2,1)S(1)} %all_gather.6, ...), dimensions={0} | concatenate | bytes 17301504 | tf_op jit(solution)/shard_map/concatenate | solution.py:86
  133.9 6.6 convert_reduce_fusion
  141.4 2.1 multiply_convert_fusion.4
  143.6 2.4 select_maximum_fusion
  147.7 7.7 %fusion.10 = (f32[128,16384]{1,0:T(8,128)}, f32[128,16384]{1,0:T(8,128)S(1)}) fusion(f32[128]{0:T(128)S(1)} %get-tuple-element.37, f32[16384]{0:T(1024)S(1)} %get-tuple-element.75, pred[16384]{0:T(1024)(128)(4,1)S(1)} %broadcast_compare_fusion.4, bf16[128,264]{0,1:T(8,128)(2,1)S(1)} %select_convert_fusion.1, bf16[264,16384]{1,0:T(8,128)(2,1)S(1)} %copy-done.1), kind=kOutput, calls=%fused_computation.23 | convolution fusion | flops 1115684864 | bytes 25577984 | tf_op jit(solution)/shard_map/dot_general | solution.py:20
  155.4 12.5 %multiply_convert_fusion = bf16[4,128,16384]{2,1,0:T(8,128)(2,1)} fusion(f32[4,16384]{1,0:T(4,128)S(1)} %fusion.53, f32[128,16384]{1,0:T(8,128)} %get-tuple-element.95), kind=kLoop, calls=%fused_computation.1 | loop fusion | flops 16777216 | bytes 25427968 | tf_op jit(solution)/shard_map/convert_element_type | solution.py:167
  167.9 10.3 %fusion.115 = (f32[512]{0:T(512)}, f32[512,264]{0,1:T(8,128)}) fusion(bf16[512,16384]{1,0:T(8,128)(2,1)} %bitcast.85, bf16[264,16384]{1,0:T(8,128)(2,1)S(1)} %copy-done.1), kind=kOutput, calls=%fused_computation.243 | convolution fusion | flops 4429319680 | bytes 25970688 | tf_op jit(solution)/shard_map/dot_general | solution.py:20
  185.6 2.7 fusion.97
  190.2 4.9 convert_reduce_fusion.2
  195.2 2.3 multiply_reduce_fusion.2
  197.5 2.7 convert_reduce_fusion.3
  202.6 14.7 %fusion.119 = f32[512,16384]{1,0:T(8,128)} fusion(bf16[512,264]{0,1:T(8,128)(2,1)S(1)} %get-tuple-element.50, bf16[264,16384]{1,0:T(8,128)(2,1)S(1)} %bitcast.79), kind=kOutput, calls=%fused_computation.247 | convolution fusion | flops 4429185024 | bytes 42475520 | tf_op jit(solution)/shard_map/dot_general | solution.py:20
  217.3 16.8 %multiply_reduce_fusion = f32[128,16384]{1,0:T(8,128)} fusion(f32[4,128,16384]{2,1,0:T(8,128)} %bitcast.80, f32[4,16384]{1,0:T(4,128)S(1)} %fusion.53), kind=kLoop, calls=%fused_computation | loop fusion | flops 14680064 | bytes 42205184 | tf_op jit(solution)/shard_map/reduce_sum | solution.py:211
  234.1 10.9 %fusion.102 = (f32[128]{0:T(128)S(1)}, f32[16384]{0:T(1024)}, bf16[128,16384]{1,0:T(8,128)(2,1)}, f32[128,16384]{1,0:T(8,128)S(1)}) fusion(f32[128,16384]{1,0:T(8,128)} %multiply_reduce_fusion, f32[16384]{0:T(1024)S(1)} %copy-done.16, f32[128,16384]{1,0:T(8,128)} %copy-done.4, f32[128]{0:T(128)S(1)} %copy-done.44, ...), kind=kOutput, calls=%fused_computation.230 | convolution fusion | flops 39894912 | bytes 29575168 | tf_op jit(solution)/shard_map/dot_general | solution.py:20
  245.0 8.9 %fusion.117 = (f32[128]{0:T(128)S(1)}, f32[128,264]{0,1:T(8,128)S(1)}) fusion(bf16[264,16384]{1,0:T(8,128)(2,1)} %concatenate.33, f32[128,16384]{1,0:T(8,128)S(1)} %get-tuple-element.104, f32[16384]{0:T(1024)S(1)} %copy-done.16), kind=kOutput, calls=%fused_computation.245 | convolution fusion | flops 1111524224 | bytes 17240576 | tf_op jit(solution)/shard_map/dot_general | solution.py:20
  254.9 5.4 fusion.96
  260.9 5.4 add_convert_fusion
  266.3 4.6 all-to-all-start
  271.8 11.5 %convert_element_type.294 = f32[264,16384]{1,0:T(8,128)} convert(bf16[264,16384]{1,0:T(8,128)(2,1)} %concatenate.33) | non-fusion elementwise | flops 4325376 | bytes 25952256 | tf_op jit(solution)/shard_map/convert_element_type | solution.py:159
  284.0 1.9 fusion.48
  285.9 5.4 fusion.94
  291.6 3.3 fusion.86
  294.9 4.2 fusion.30
  307.0 5.1 copy.41
  313.6 56.1 %all-reduce.9 = (bf16[264,1024]{1,0:T(8,128)(2,1)}, f32[1024]{0:T(1024)S(1)}, f32[1024]{0:T(1024)}, f32[1024]{0:T(1024)}, f32[1024]{0:T(1024)}, /*index=5*/f32[1024]{0:T(1024)}, f32[264]{0:T(512)S(1)}, f32[264]{0:T(512)S(1)}) all-reduce(f32[264,1024]{1,0:T(8,128)} %fusion.86, ...), channel_id=1, replica_groups=mesh['dp'=8,'pix'=4] {'dp','pix'}, use_global_device_ids=true, to_apply=%region_24.25 | all-reduce | flops 275984 | bytes 1667200 | tf_op jit(solution)/shard_map/psum | solution.py:233
  369.7 3.0 fusion.121
  376.0 2.6 reduce_sum.303
  378.6 2.9 bitcast_convert_fusion.1
  381.5 1.9 convolution_add_fusion
  383.5 2.5 pad_maximum_fusion.1
  385.9 16.4 %all_gather.7 = f32[512,265]{0,1:T(8,128)S(1)} all-gather(f32[128,265]{0,1:T(8,128)} %all-reduce.8.cloned.1.call-done), channel_id=1, replica_groups=mesh['dp'=8,'pix'=4] {'pix'}, dimensions={0}, use_global_device_ids=true | all-gather | bytes 678400 | tf_op jit(solution)/shard_map/all_gather | solution.py:237
  402.4 2.0 multiply_reduce_fusion.10
  407.1 2.5 multiply_reduce_fusion.8
  409.6 5.6 fusion.103
  416.7 6.9 %reduce-scatter.15.cloned.1.call-done = f32[1024,128]{1,0:T(8,128)} async-done(((f32[1024,1024]{1,0:T(8,128)}), f32[1024,128]{1,0:T(8,128)}) %reduce-scatter.15.cloned.1.call-update) | async-done | bytes 524304 | tf_op jit(solution)/shard_map/reduce_scatter | solution.py:228
  425.0 1.9 fusion.51
  429.3 141.1 %reduce-scatter.19.cloned.1.call-done = f32[4096,3]{1,0:T(8,128)} async-done(((f32[16384,3]{1,0:T(8,128)}), f32[4096,3]{1,0:T(8,128)}) %reduce-scatter.19.cloned.1.call-update) | async-done | bytes 49168
  570.3 2.8 copy.42
  573.2 34.9 %reduce-scatter.9.cloned.1.call-done = f32[128,128]{1,0:T(8,128)} async-done(((f32[128,1024]{1,0:T(8,128)}), f32[128,128]{1,0:T(8,128)}) %reduce-scatter.9.cloned.1.call-update) | async-done | bytes 65552 | tf_op jit(solution)/shard_map/reduce_scatter | solution.py:226
  609.8 22.8 %reduce-scatter.13.cloned.1.call-done = f32[256,128]{1,0:T(8,128)} async-done(((f32[1024,128]{1,0:T(8,128)}), f32[256,128]{1,0:T(8,128)}) %reduce-scatter.13.cloned.1.call-update) | async-done | bytes 131088 | tf_op jit(solution)/shard_map/reduce_scatter | solution.py:230
  632.6 22.9 %reduce-scatter.17.cloned.1.call-done = f32[256,128]{1,0:T(8,128)} async-done(((f32[1024,128]{1,0:T(8,128)}), f32[256,128]{1,0:T(8,128)}) %reduce-scatter.17.cloned.1.call-update) | async-done | bytes 131088 | tf_op jit(solution)/shard_map/reduce_scatter | solution.py:227
  (255 shorter events, 46.1 us)
Async XLA Ops:
  7.2 134.2 %copy-start = (bf16[1024,1024]{1,0:T(8,128)(2,1)S(1)}, bf16[1024,1024]{1,0:T(8,128)(2,1)}, u32[]{:S(2)}) copy-start(bf16[1024,1024]{1,0:T(8,128)(2,1)} %param.28) | copy-start | bytes 6291460
  7.2 9.4 %copy-start.39 = (s32[2,4]{1,0:T(2,128)S(1)}, s32[2,4]{1,0:T(2,128)}, u32[]{:S(2)}) copy-start(s32[2,4]{1,0:T(2,128)} %param.25) | copy-start | bytes 100
  7.2 33.3 %copy-start.58 = (f32[261]{0:T(512)S(1)}, f32[261]{0:T(512)}, u32[]{:S(2)}) copy-start(f32[261]{0:T(512)} %param.26) | copy-start | bytes 3136
  7.2 33.9 %copy-start.59 = (f32[261]{0:T(512)S(1)}, f32[261]{0:T(512)}, u32[]{:S(2)}) copy-start(f32[261]{0:T(512)} %param.27) | copy-start | bytes 3136
  10.1 35.2 %copy-start.10 = (bf16[512,1024]{1,0:T(8,128)(2,1)S(1)}, bf16[512,1024]{1,0:T(8,128)(2,1)}, u32[]{:S(2)}) copy-start(bf16[512,1024]{1,0:T(8,128)(2,1)} %param.23) | copy-start | bytes 3145732
  10.1 178.2 %all-to-all-start.1 = ((bf16[4,128,1024]{2,1,0:T(8,128)(2,1)}), bf16[4,128,1024]{2,1,0:T(8,128)(2,1)}, u32[]{:S(2)}, u32[]{:S(2)}) async-start(bf16[4,128,1024]{2,1,0:T(8,128)(2,1)} %bitcast.86), calls=%async_computation.1 | async-start | bytes 2097152 | tf_op jit(solution)/shard_map/all_to_all | solution.py:140
  16.6 369.4 %all-reduce.8.cloned.1.call-start = ((), (), s32[]{:S(2)}) async-start(), calls=%async_computation.9 | async-start | bytes 278528 | tf_op jit(solution)/shard_map/psum | solution.py:236
  44.5 101.5 %copy-start.40 = (bf16[4,1024]{1,0:T(4,128)(2,1)}, bf16[4,1024]{1,0:T(4,128)(2,1)S(1)}, u32[]{:S(2)}) copy-start(bf16[4,1024]{1,0:T(4,128)(2,1)S(1)} %slice.178) | copy-start | bytes 24580
  45.2 100.8 %copy-start.55 = (bf16[1,1024]{1,0:T(2,128)(2,1)}, bf16[1,1024]{1,0:T(2,128)(2,1)S(1)}, u32[]{:S(2)}) copy-start(bf16[1,1024]{1,0:T(2,128)(2,1)S(1)} %slice.179) | copy-start | bytes 6148
  45.3 101.1 %copy-start.19 = (s32[16384]{0:T(1024)}, s32[16384]{0:T(1024)S(1)}, u32[]{:S(2)}) copy-start(s32[16384]{0:T(1024)S(1)} %convert_add_fusion) | copy-start | bytes 196612
  133.9 7.0 %copy-start.47 = (f32[1024]{0:T(1024)S(1)}, f32[1024]{0:T(1024)}, u32[]{:S(2)}) copy-start(f32[1024]{0:T(1024)} %param.36) | copy-start | bytes 12292
  133.9 7.0 %copy-start.48 = (f32[1024]{0:T(1024)S(1)}, f32[1024]{0:T(1024)}, u32[]{:S(2)}) copy-start(f32[1024]{0:T(1024)} %param.35) | copy-start | bytes 12292
  140.9 5.1 copy-start.34
  140.9 5.1 copy-start.36
  141.4 6.3 copy-start.1
  146.4 9.0 %copy-start.42 = (f32[128]{0:T(128)}, f32[128]{0:T(128)S(1)}, u32[]{:S(2)}) copy-start(f32[128]{0:T(128)S(1)} %get-tuple-element.37) | copy-start | bytes 1540
  147.6 7.8 %copy-start.15 = (f32[16384]{0:T(1024)}, f32[16384]{0:T(1024)S(1)}, u32[]{:S(2)}) copy-start(f32[16384]{0:T(1024)S(1)} %get-tuple-element.75) | copy-start | bytes 196612
  147.7 7.7 %copy-start.29 = (bf16[128,264]{0,1:T(8,128)(2,1)}, bf16[128,264]{0,1:T(8,128)(2,1)S(1)}, u32[]{:S(2)}) copy-start(bf16[128,264]{0,1:T(8,128)(2,1)S(1)} %select_convert_fusion.1) | copy-start | bytes 202756
  155.4 26.5 %copy-start.4 = (f32[128,16384]{1,0:T(8,128)}, f32[128,16384]{1,0:T(8,128)S(1)}, u32[]{:S(2)}) copy-start(f32[128,16384]{1,0:T(8,128)S(1)} %get-tuple-element.96) | copy-start | bytes 25165828
  167.9 12.1 %copy-start.5 = (bf16[1024,1024]{1,0:T(8,128)(2,1)S(1)}, bf16[1024,1024]{1,0:T(8,128)(2,1)}, u32[]{:S(2)}) copy-start(bf16[1024,1024]{1,0:T(8,128)(2,1)} %param.33) | copy-start | bytes 6291460
  190.2 4.9 copy-start.23
  190.2 4.9 copy-start.9
  190.2 4.9 copy-start.61
  195.2 7.4 %slice-start = ((s8[8650752]{0:T(1024)(128)(4,1)}), s8[4194304]{0:T(1024)(128)(4,1)S(1)}, s32[]{:S(2)}) async-start(s8[8650752]{0:T(1024)(128)(4,1)} %bitcast.78), calls=%async_computation.15 | async-start | bytes 8388608
  195.2 7.4 %slice-start.1 = ((s8[8650752]{0:T(1024)(128)(4,1)}), s8[4194304]{0:T(1024)(128)(4,1)S(1)}, s32[]{:S(2)}) async-start(s8[8650752]{0:T(1024)(128)(4,1)} %bitcast.78), calls=%async_computation.16 | async-start | bytes 8388608
  197.5 5.1 slice-start.2
  202.6 14.7 %copy-start.18 = (bf16[512,264]{0,1:T(8,128)(2,1)}, bf16[512,264]{0,1:T(8,128)(2,1)S(1)}, u32[]{:S(2)}) copy-start(bf16[512,264]{0,1:T(8,128)(2,1)S(1)} %get-tuple-element.50) | copy-start | bytes 811012
  217.3 16.8 %copy-start.16 = (f32[16384]{0:T(1024)S(1)}, f32[16384]{0:T(1024)}, u32[]{:S(2)}) copy-start(f32[16384]{0:T(1024)} %copy-done.15) | copy-start | bytes 196612
  217.3 16.8 %copy-start.44 = (f32[128]{0:T(128)S(1)}, f32[128]{0:T(128)}, u32[]{:S(2)}) copy-start(f32[128]{0:T(128)} %copy-done.42) | copy-start | bytes 1540
  245.0 9.0 %copy-start.2 = (f32[128,16384]{1,0:T(8,128)}, f32[128,16384]{1,0:T(8,128)S(1)}, u32[]{:S(2)}) copy-start(f32[128,16384]{1,0:T(8,128)S(1)} %get-tuple-element.104) | copy-start | bytes 25165828
  245.0 9.8 %copy-start.46 = (f32[1024]{0:T(1024)S(1)}, f32[1024]{0:T(1024)}, u32[]{:S(2)}) copy-start(f32[1024]{0:T(1024)} %param.37) | copy-start | bytes 12292
  245.0 9.8 %copy-start.64 = (f32[1024]{0:T(1024)S(1)}, f32[1024]{0:T(1024)}, u32[]{:S(2)}) copy-start(f32[1024]{0:T(1024)} %param.38) | copy-start | bytes 12292
  254.8 154.8 %reduce-scatter.11.cloned.1.call-start = ((), (), s32[]{:S(2)}) async-start(), calls=%async_computation.10 | async-start | bytes 4718592 | tf_op jit(solution)/shard_map/reduce_scatter | solution.py:231
  266.3 112.3 %all-to-all-start = ((bf16[4,128,1024]{2,1,0:T(8,128)(2,1)}), bf16[4,128,1024]{2,1,0:T(8,128)(2,1)}, u32[]{:S(2)}, u32[]{:S(2)}) async-start(bf16[4,128,1024]{2,1,0:T(8,128)(2,1)} %bitcast.88), calls=%async_computation | async-start | bytes 2097152 | tf_op jit(solution)/shard_map/all_to_all | solution.py:184
  270.9 152.7 %reduce-scatter.15.cloned.1.call-start = ((), (), s32[]{:S(2)}) async-start(), calls=%async_computation.12 | async-start | bytes 4718592 | tf_op jit(solution)/shard_map/reduce_scatter | solution.py:228
  291.3 279.0 %reduce-scatter.19.cloned.1.call-start = ((), (), s32[]{:S(2)}) async-start(), calls=%async_computation.14 | async-start | bytes 10485760
  294.9 4.6 copy-start.3
  294.9 9.0 %slice-start.3 = ((s8[8388608]{0:T(1024)(128)(4,1)}), s8[4194304]{0:T(1024)(128)(4,1)S(1)}, s32[]{:S(2)}) async-start(s8[8388608]{0:T(1024)(128)(4,1)} %bitcast.81), calls=%async_computation.18 | async-start | bytes 8388608
  312.1 296.0 %reduce-scatter.9.cloned.1.call-start = ((), (), s32[]{:S(2)}) async-start(), calls=%async_computation.8 | async-start | bytes 589824 | tf_op jit(solution)/shard_map/reduce_scatter | solution.py:226
  369.7 6.2 copy-start.50
  378.6 4.9 slice-start.5
  381.4 20.9 %copy-start.35 = (bf16[128,1024]{1,0:T(8,128)(2,1)S(1)}, bf16[128,1024]{1,0:T(8,128)(2,1)}, u32[]{:S(2)}) copy-start(bf16[128,1024]{1,0:T(8,128)(2,1)} %get-tuple-element.62) | copy-start | bytes 786436
  381.4 20.9 %copy-start.41 = (bf16[4,1024]{1,0:T(4,128)(2,1)S(1)}, bf16[4,1024]{1,0:T(4,128)(2,1)}, u32[]{:S(2)}) copy-start(bf16[4,1024]{1,0:T(4,128)(2,1)} %copy-done.40) | copy-start | bytes 24580
  381.4 20.9 %copy-start.56 = (bf16[1,1024]{1,0:T(2,128)(2,1)S(1)}, bf16[1,1024]{1,0:T(2,128)(2,1)}, u32[]{:S(2)}) copy-start(bf16[1,1024]{1,0:T(2,128)(2,1)} %copy-done.55) | copy-start | bytes 6148
  381.5 251.1 %reduce-scatter.13.cloned.1.call-start = ((), (), s32[]{:S(2)}) async-start(), calls=%async_computation.11 | async-start | bytes 655360 | tf_op jit(solution)/shard_map/reduce_scatter | solution.py:230
  409.6 245.9 %reduce-scatter.17.cloned.1.call-start = ((), (), s32[]{:S(2)}) async-start(), calls=%async_computation.13 | async-start | bytes 655360 | tf_op jit(solution)/shard_map/reduce_scatter | solution.py:227
  415.2 12.9 %slice-start.6 = ((f32[264,1024]{1,0:T(8,128)}), f32[4,1024]{1,0:T(4,128)S(1)}, s32[]{:S(2)}) async-start(f32[264,1024]{1,0:T(8,128)} %copy-done.14), calls=%async_computation.21 | async-start | bytes 32768 | tf_op jit(solution)/shard_map/slice | solution.py:46
  428.2 180.0 %copy-start.57 = (f32[128]{0:T(128)S(1)}, f32[128]{0:T(128)}, u32[]{:S(2)}) copy-start(f32[128]{0:T(128)} %dynamic-slice.2) | copy-start | bytes 1540
  (39 other events, 79.7 us)
Sparse Core Ops, SparseCore 0:
  254.9 52.7 all-reduce.7
  311.0 56.9 reduce-scatter.10
  371.7 51.8 reduce-scatter.14
  425.8 144.4 reduce-scatter.18
  573.3 34.8 reduce-scatter.8
  610.9 21.6 reduce-scatter.12
  635.5 19.9 reduce-scatter.16

commit v2 on v1

v2 whole, which is shorter than its diff:
```python
from functools import partial
import math
from types import SimpleNamespace

import jax
import jax.numpy as jnp
from jax import lax
from jax.experimental import pallas as pl
from jax.experimental.pallas import tpu as pltpu
from jax.sharding import PartitionSpec as P

BANDS = 64
MAXRES = 224
BIG_SIDE = 112
SMALL_SIDE = 32
EPSILON = 1e-05
FEAT = 4 * BANDS + 5
WIDE = FEAT + 11
DQ = 384
PACK = 320
TILE = 512
LANES = 128
MESH = pl.DeviceIdType.MESH
SENDS = 49
VMEM_LIMIT = 62 * 2**20

bf16 = jnp.bfloat16
f32 = jnp.float32


def dot(a, b, dims):
    return lax.dot_general(a, b, (dims, ((), ())), preferred_element_type=f32)


def nn(a, b):
    return dot(a, b, ((1,), (0,)))


def nt(a, b):
    return dot(a, b, ((1,), (1,)))


def tn(a, b):
    return dot(a, b, ((0,), (0,)))


def order_of(rows, cols, flip=False):
    b = 2 * BANDS
    f = lax.broadcasted_iota(jnp.int32, (rows, cols), 1 if flip else 0)
    g = lax.broadcasted_iota(jnp.int32, (rows, cols), 0 if flip else 1)
    to = jnp.where(f < 4, f + 2 * b, jnp.where(f < 4 + b, f - 4, jnp.where(f == 4 + b, 2 * b + 4, f - 5)))
    return ((to == g) & (f < FEAT)).astype(bf16)


def moved(rows, order, product):
    total = None
    for _ in range(3):
        part = rows.astype(bf16)
        rows = rows - part.astype(f32)
        piece = product(part, order)
        total = piece if total is None else total + piece
    return total


def centred(rows, axis):
    live = lax.broadcasted_iota(jnp.int32, rows.shape, axis) < FEAT
    rows = jnp.where(live, rows, 0.0)
    return jnp.where(live, rows - jnp.sum(rows, axis=axis, keepdims=True) * (1.0 / FEAT), 0.0)


def norm(rows):
    centre = rows - jnp.mean(rows, axis=-1, keepdims=True)
    scale = lax.rsqrt(jnp.mean(centre * centre, axis=-1, keepdims=True) + EPSILON)
    return centre * scale, scale


def norm_back(grad, unit, scale):
    return (
        grad
        - jnp.mean(grad, axis=-1, keepdims=True)
        - unit * jnp.mean(grad * unit, axis=-1, keepdims=True)
    ) * scale


def tanh(a):
    return 1.0 - 2.0 / (1.0 + jnp.exp(jnp.minimum(2.0 * a, 80.0)))


def sin_cos_pi(p):
    n = jnp.floor(p + 0.5)
    z = (p - n) * math.pi
    q = z * z
    s = z * (1.0 + q * (-1.0 / 6 + q * (1.0 / 120 + q * (-1.0 / 5040 + q * (1.0 / 362880 - q * (1.0 / 39916800))))))
    c = 1.0 + q * (
        -0.5 + q * (1.0 / 24 + q * (-1.0 / 720 + q * (1.0 / 40320 + q * (-1.0 / 3628800 + q * (1.0 / 479001600)))))
    )
    sign = 1.0 - 2.0 * (n - 2.0 * jnp.floor(n * 0.5))
    return s * sign, c * sign


def tiles_of(images, slots):
    spare = (images - 1) * SMALL_SIDE * SMALL_SIDE
    head = -(-spare // TILE)
    tail = BIG_SIDE * BIG_SIDE // TILE
    last = min(-(-(BIG_SIDE * BIG_SIDE + spare) // TILE), slots // TILE)
    return head, max(head, tail), last


def loop(lo, hi, body, unroll):
    steps = (hi - lo) // unroll
    if steps > 0:
        lax.fori_loop(0, steps, lambda i, c: (body([lo + i * unroll + k for k in range(unroll)]), c)[1], 0)
    if lo + steps * unroll < hi:
        body(list(range(lo + steps * unroll, hi)))


def wait(copies):
    for copy in copies:
        copy.wait()


def summed(first, others):
    total = first.astype(f32)
    for i in range(others.shape[0]):
        total = total + others[i].astype(f32)
    return total


MLP_UNROLL = 2
HEAD_UNROLL = 2
BIG_UNROLL = 3


def layer_kernel(images, slots, parts, fused, names, *refs):
    r = SimpleNamespace(**dict(zip(names, refs)))
    group, place = lax.axis_index("dp"), lax.axis_index("pix")
    count, width = r.latents.shape
    own, chunk = count // parts, width // parts
    rows_all = images * own
    head, tail, last = tiles_of(images, slots)
    per = r.rgb_in.shape[0] // 4
    factor = 1.0 / math.sqrt(width)
    core, quad = lax.rem(group, 2), lax.rem(group // 2, 4)
    base = group // 8 * 4
    x, y = lax.rem(quad, 2), quad // 2
    mate = ((base + quad) * 2 + 1 - core, place)

    def away(k):
        other = (1 - x if k % 2 else x) + 2 * (1 - y if k // 2 else y)
        return other, ((base + other) * 2 + core, place)

    zs = [(s, lax.rem(place + s, parts), lax.rem(place + parts - s, parts)) for s in range(1, parts)]
    used = [0]

    def send(src, dst, target):
        i = used[0]
        used[0] += 1
        copy = pltpu.make_async_remote_copy(
            src_ref=src, dst_ref=dst, send_sem=r.sems.at[0, i], recv_sem=r.sems.at[1, i],
            device_id=target, device_id_type=MESH,
        )
        copy.start()
        return copy

    def send_z(pick, put):
        return [send(pick(to), put(s), (group, to)) for s, to, _ in zs]

    def send_quad(pick, put):
        return [send(pick(away(k)[0]), put(k), away(k)[1]) for k in (1, 2, 3)]

    loads = [
        pltpu.make_async_copy(a, b, r.load_sems.at[i])
        for i, (a, b) in enumerate(
            ((r.cot_h, r.cot_f), (r.wq_h, r.wq), (r.wo_h, r.wo), (r.up_h, r.up), (r.down_h, r.down))
        )
    ]
    for copy in loads:
        copy.start()

    barrier = pltpu.get_barrier_semaphore()
    friends = [(group, to) for _, to, _ in zs]
    if fused:
        friends += [mate] + [away(k)[1] for k in (1, 2, 3)]
    for device in friends:
        pl.semaphore_signal(barrier, inc=1, device_id=device, device_id_type=MESH)
    pl.semaphore_wait(barrier, len(friends))

    rgb_copies = send_z(lambda to: r.rgb_in, lambda s: r.rgb_recv.at[s - 1])
    loads[0].wait()
    r.cot_send[...] = r.cot_f[0].astype(bf16).reshape(parts, own, width)
    cot_copies = send_z(lambda to: r.cot_send.at[to], lambda s: r.cot_low.at[place])
    r.cot_low[place] = r.cot_send[place]

    to_waves = order_of(WIDE, FEAT, flip=True)
    r.wk[:WIDE] = nn(to_waves, r.wk_in[...]).astype(bf16)
    r.wk[WIDE:] = jnp.zeros_like(r.wk[WIDE:])
    vb = r.vecs[10:11, :]
    vb_high = vb.astype(bf16).astype(f32)
    row = lax.broadcasted_iota(jnp.int32, (WIDE, width), 0)
    wv = nn(to_waves, r.wv_in[...])
    r.wv[...] = jnp.where(row == FEAT, vb_high, jnp.where(row == FEAT + 1, vb - vb_high, wv)).astype(bf16)
    feats = moved(r.vecs[8:16, :DQ], order_of(DQ, DQ), nn)
    r.feats[...] = feats
    gain, bias = feats[0:1, :WIDE], feats[1:2, :WIDE]

    loads[1].wait()
    rows = pl.ds(pl.multiple_of(place * own, own), own)
    lat_rows = r.latents[rows, :].astype(f32)
    own_unit, _ = norm(lat_rows)
    own_in = (own_unit * r.vecs[2:3, :] + r.vecs[3:4, :]).astype(bf16)
    own_queries = ((nn(own_in, r.wq[...]) + r.vecs[0:1, :]) * factor).astype(bf16)
    qk = nt(own_queries, r.wk[:WIDE])
    qc = centred(qk * gain, 1).astype(bf16)
    r.qc[...] = qc
    r.qb[...] = jnp.sum(qk * bias, axis=1, keepdims=True)
    pick = (
        lax.broadcasted_iota(jnp.int32, (16, WIDE), 1)
        == lax.broadcasted_iota(jnp.int32, (16, WIDE), 0) + 4 * BANDS
    ).astype(bf16)
    r.ext[images * 16 :, :] = nt(pick, qc).astype(bf16)

    wait(rgb_copies)
    for c in range(3):
        at = slice(c * per, (c + 1) * per)
        r.rgbf[c, pl.ds(pl.multiple_of(place * per, per), per), :] = r.rgb_in[at, :].astype(f32)
        for s, _, source in zs:
            r.rgbf[c, pl.ds(pl.multiple_of(source * per, per), per), :] = r.rgb_recv[s - 1, at, :].astype(f32)

    ends, high, wide = [], [], []
    end = jnp.int32(0)
    for i in range(images):
        end = end + r.sizes[0, i] * r.sizes[1, i]
        ends.append(end.astype(f32))
        high.append(jnp.maximum(r.sizes[0, i] - 1, 1).astype(f32))
        wide.append(r.sizes[1, i].astype(f32))
    is_big = [(r.sizes[0, n] > SMALL_SIDE).astype(f32) for n in range(images)]

    def features(j):
        shape = (8, TILE)
        lane = lax.broadcasted_iota(jnp.int32, shape, 1)
        sub = lax.broadcasted_iota(jnp.int32, shape, 0)
        slot = (lane + j * TILE).astype(f32)
        segment = jnp.zeros(shape, f32)
        start = jnp.zeros(shape, f32)
        tall = jnp.full(shape, high[0])
        across = jnp.full(shape, wide[0])
        for i in range(images):
            past = slot >= ends[i]
            segment = jnp.where(past, segment + 1.0, segment)
            if i + 1 < images:
                start = jnp.where(past, ends[i], start)
                tall = jnp.where(past, high[i + 1], tall)
                across = jnp.where(past, wide[i + 1], across)
            else:
                start = jnp.where(past, slot, start)
        local = slot - start
        row = jnp.floor((local + 0.5) / across)
        col = local - row * across
        y = 2.0 * row / tall - 1.0
        x = 2.0 * col / jnp.maximum(across - 1.0, 1.0) - 1.0
        step = (MAXRES / 2.0 - 1.0) / (BANDS - 1)
        lowest = 1.0 + sub.astype(f32) * step
        total = None
        pieces = []
        for spot in (y, x):
            s, c = sin_cos_pi(lowest * spot)
            rs, rc = sin_cos_pi((8 * step) * spot)
            sines, cosines = [s], [c]
            for _ in range(BANDS // 8 - 1):
                s, c = s * rc + c * rs, c * rc - s * rs
                sines.append(s)
                cosines.append(c)
            for k in range(BANDS // 8):
                total = sines[k] + cosines[k] if total is None else total + (sines[k] + cosines[k])
            pieces.append(jnp.concatenate(sines, axis=0).astype(bf16))
            pieces.append(jnp.concatenate(cosines, axis=0).astype(bf16))
        total = jnp.sum(total, axis=0, keepdims=True)
        red, green, blue = (r.rgbf[c, pl.ds(j, 1), :] for c in range(3))
        y, x, segment = y[0:1], x[0:1], segment[0:1]
        total = total + (red + green + blue + y + x)
        squares = red * red + green * green + blue * blue + y * y + x * x + 2.0 * BANDS
        mean = total * (1.0 / FEAT)
        spread = squares * (1.0 / FEAT) - mean * mean + EPSILON
        scale = lax.rsqrt(spread)
        deviation = spread * scale
        rest = deviation - deviation.astype(bf16).astype(f32)
        ext = jnp.zeros(shape, f32)
        for k, v in enumerate((red, green, blue, y, x, deviation, rest)):
            ext = jnp.where(sub == k, v, ext)
        pieces.append(jnp.concatenate([ext, jnp.zeros(shape, f32)], axis=0).astype(bf16))
        tile = jnp.concatenate(pieces, axis=0)
        r.feat[j] = tile
        r.stat[j] = jnp.where(sub == 0, scale, jnp.where(sub == 1, mean, segment))
        return tile, scale, segment

    r.acc[...] = jnp.zeros_like(r.acc)
    r.acc_big[...] = jnp.zeros_like(r.acc_big)

    def side(parts_of):
        return parts_of[0] if len(parts_of) == 1 else jnp.concatenate(parts_of, axis=1)

    def forward(mixed, js):
        tiles, mixes = [], []
        for j in js:
            tile, scale, segment = features(j)
            weights = jnp.exp(nn(r.qc[...], tile) * scale + r.qb[...])
            if mixed:
                weights = jnp.where(segment < images, weights, 0.0)
            r.wst[j] = weights.astype(bf16)
            scaled = (weights * scale).astype(bf16)
            if mixed:
                none = jnp.zeros_like(scaled)
                scaled = jnp.concatenate([jnp.where(segment == n, scaled, none) for n in range(images)], axis=0)
            tiles.append(tile)
            mixes.append(scaled)
        into = r.acc if mixed else r.acc_big
        into[...] += nt(side(tiles), side(mixes))

    loop(0, head, partial(forward, True), HEAD_UNROLL)
    loop(head, tail, partial(forward, False), BIG_UNROLL)
    loop(tail, last, partial(forward, True), HEAD_UNROLL)

    loads[2].wait()
    wvo = nn(r.wv[...], r.wo[...])
    const = wvo[FEAT : FEAT + 1] + wvo[FEAT + 1 : FEAT + 2] + r.vecs[1:2, :]
    r.wvo[...] = jnp.where(row < FEAT, wvo, 0.0).astype(bf16)
    lane = lax.broadcasted_iota(jnp.int32, (own, WIDE), 1)
    ones = ((lane == FEAT) | (lane == FEAT + 1)).astype(f32)
    big = r.acc_big[...]
    mix_all = (r.acc[...] + jnp.concatenate([big * is_big[n] for n in range(images)], axis=1)).T
    for n in range(images):
        at = slice(n * own, (n + 1) * own)
        mix = mix_all[at]
        totals = mix[:, FEAT : FEAT + 1] + mix[:, FEAT + 1 : FEAT + 2]
        unit = centred(mix, 1) / totals
        r.tot[at, :] = totals
        r.unit[at, :] = unit
        r.px[at, :] = (unit * gain + bias + ones).astype(bf16)

    loads[3].wait()
    loads[4].wait()
    k = math.sqrt(2.0 / math.pi)
    half = 2 * own
    out_copies = []
    for blk in range(rows_all // half):
        at = slice(blk * half, (blk + 1) * half)
        px = r.px[at, :]
        middle = jnp.concatenate([lat_rows] * (half // own), axis=0) + nn(px, r.wvo[...]) + const
        mid_unit, mid_scale = norm(middle)
        mid_in = (mid_unit * r.vecs[4:5, :] + r.vecs[5:6, :]).astype(bf16)
        hidden = nn(mid_in, r.up[...]) + r.vecs[6:7, :]
        th = tanh(k * (hidden + 0.044715 * hidden * hidden * hidden))
        active = (0.5 * hidden * (1.0 + th)).astype(bf16)
        r.cot_f[0, at, :] = 0.5 * (1.0 + th) + 0.5 * hidden * (1.0 - th * th) * k * (
            1.0 + 3 * 0.044715 * hidden * hidden
        )
        done = (middle + nn(active, r.down[...]) + r.vecs[7:8, :]).astype(bf16)
        r.out_send[2 * blk] = done[:own]
        r.out_send[2 * blk + 1] = done[own:]
        r.mid_unit[at, :] = mid_unit
        r.mid_scale[at, :] = mid_scale
        r.act_t[:, at] = active.T
        r.mid_t[:, at] = mid_in.T
        r.px_t[:, at] = px.T
    out_copies = send_z(lambda to: r.out_send.at[to], lambda s: r.out_rows.at[place])
    r.out_rows[place] = r.out_send[place]

    wait(cot_copies)

    def down_grads(jj, c):
        cols = pl.ds(pl.multiple_of(jj * 256, 256), 256)
        grads = jnp.concatenate([r.cot_low[n, :, cols] for n in range(images)], axis=0)
        part = nn(r.act_t[...], grads).astype(bf16)
        for i in range(2):
            r.down_pay[i, lax.rem(jj, 2) * 2 + jj // 2] = part[:, i * LANES : (i + 1) * LANES]
        return c

    lax.fori_loop(0, width // 256, down_grads, 0)
    if fused:
        core_down = send(r.down_pay.at[1 - core], r.down_c, mate)

    total_sums, lat_sum, ext_total = None, None, None
    for blk in range(rows_all // half):
        at = slice(blk * half, (blk + 1) * half)
        grad_down = r.cot_low[2 * blk : 2 * blk + 2].reshape(half, width)
        grad_hidden = (r.cot_f[0, at, :] * nt(grad_down, r.down[...])).astype(bf16)
        r.gh[at, :] = grad_hidden
        grad_mid = nt(grad_hidden, r.up[...])
        mid_unit = r.mid_unit[at, :]
        cot = grad_down.astype(f32)
        grad_middle = cot + norm_back(grad_mid * r.vecs[4:5, :], mid_unit, r.mid_scale[at, :])
        branch = grad_middle.astype(bf16)
        r.branch[at, :] = branch
        part = [
            jnp.sum(v, axis=0, keepdims=True)
            for v in (cot, grad_hidden.astype(f32), branch.astype(f32), grad_mid * mid_unit, grad_mid)
        ]
        total_sums = part if total_sums is None else [u + v for u, v in zip(total_sums, part)]
        both = grad_middle[:own] + grad_middle[own:]
        lat_sum = both if lat_sum is None else lat_sum + both
        gx = nt(branch, r.wvo[...])
        r.gx[at, :] = gx
        part = [jnp.sum(gx * r.unit[at, :], axis=0, keepdims=True), jnp.sum(gx, axis=0, keepdims=True)]
        ext_total = part if ext_total is None else [u + v for u, v in zip(ext_total, part)]
    small = jnp.concatenate(
        total_sums
        + [jnp.pad(v, ((0, 0), (0, width - WIDE))) for v in ext_total]
        + [jnp.zeros((PACK - WIDE - 7, width), f32)],
        axis=0,
    ).astype(bf16)
    lat_low = lat_sum.astype(bf16)
    for d in range(width // LANES):
        cols = slice(d * LANES, (d + 1) * LANES)
        r.pack[d % 2, d // 2, WIDE:, :] = small[:, cols]
        r.up_pay[d % 2, d // 2, width:, :] = lat_low[:, cols]

    if fused:
        core_down.wait()
        for b in range(4):
            r.down_c[b] = r.down_c[b] + r.down_pay[core, b]
        first_down = send(r.down_c.at[pl.ds((1 - x) * 2, 2)], r.down_1, away(1)[1])

    def moments(jj, c):
        cols = pl.ds(pl.multiple_of(jj * 256, 256), 256)
        part = nn(r.px_t[...], r.branch[:, cols]).astype(bf16)
        for i in range(2):
            r.pack[i, jj, :WIDE] = part[:, i * LANES : (i + 1) * LANES]
        return c

    def up_grads(jj, c):
        cols = pl.ds(pl.multiple_of(jj * 256, 256), 256)
        part = nn(r.mid_t[...], r.gh[:, cols]).astype(bf16)
        for i in range(2):
            r.up_pay[i, jj, :width] = part[:, i * LANES : (i + 1) * LANES]
        return c

    lax.fori_loop(0, width // 256, moments, 0)
    if fused:
        core_pack = send(r.pack.at[1 - core], r.pack_c, mate)
    lax.fori_loop(0, width // 256, up_grads, 0)
    if fused:
        core_up = send(r.up_pay.at[1 - core], r.up_c, mate)

    gcb = jnp.zeros((own, WIDE), f32)
    levb = jnp.zeros((own, 1), f32)
    for n in range(images):
        at = slice(n * own, (n + 1) * own)
        gc = centred(r.gx[at, :] / r.tot[at, :] * gain, 1)
        gc_low = gc.astype(bf16)
        level = jnp.sum(gc_low.astype(f32) * r.unit[at, :], axis=1, keepdims=True)
        r.gc[at, :] = gc_low
        r.lev[at, :] = level
        r.ext[n * 16 : (n + 1) * 16, :] = nt(pick, gc_low).astype(bf16)
        gcb = gcb + gc * is_big[n]
        levb = levb + level * is_big[n]
    r.gcb[...] = gcb.astype(bf16)
    r.levb[...] = levb
    r.extb[:, own:] = nt(pick, r.gcb[...]).astype(bf16)
    r.extb[:, :own] = r.ext[images * 16 :, :]

    if fused:
        core_pack.wait()
        r.pack_c[...] = r.pack_c[...] + r.pack[core]
        quad_pack = send_quad(lambda q: r.pack_c.at[q], lambda k: r.pack_q.at[k - 1])
        core_up.wait()
        for b in range(4):
            r.up_c[b] = r.up_c[b] + r.up_pay[core, b]
        first_up = send(r.up_c.at[pl.ds((1 - y) * 2, 2)], r.up_1, away(2)[1])

    r.dq_sum[...] = jnp.zeros_like(r.dq_sum)
    r.rgbp[...] = jnp.zeros_like(r.rgbp)

    def backward(mixed, js):
        tiles, grads = [], []
        for j in js:
            tile = r.feat[j]
            scale = r.stat[j, 0:1, :]
            mean = r.stat[j, 1:2, :]
            low_weights = r.wst[j]
            weights = low_weights.astype(f32)
            raw = nn(r.qc[...], tile) * scale
            if mixed:
                segment = r.stat[j, 2:3, :]
                pulls = nn(r.gc[...], tile)
                pull = jnp.zeros_like(weights)
                level = jnp.zeros_like(weights)
                for n in range(images):
                    at = slice(n * own, (n + 1) * own)
                    here = segment == n
                    pull = jnp.where(here, pulls[at], pull)
                    level = jnp.where(here, r.lev[at, :], level)
            else:
                pull = nn(r.gcb[...], tile)
                level = r.levb[...]
            pull = pull * scale
            grad = weights * (pull - level)
            lean = jnp.sum(grad * raw + weights * pull, axis=0, keepdims=True) * (1.0 / FEAT)
            if mixed:
                colours = nn(r.ext[: images * 16, :], low_weights)
                back = nn(r.ext[images * 16 :, :], grad.astype(bf16))
                picked = jnp.zeros_like(back)
                for n in range(images):
                    picked = jnp.where(segment == n, colours[n * 16 : (n + 1) * 16], picked)
                back = back + picked
            else:
                back = nn(r.extb[...], jnp.concatenate([grad.astype(bf16), low_weights], axis=0))
            ext = tile[4 * BANDS :, :].astype(f32)
            part = (back - (ext - mean) * scale * lean) * scale
            for c in range(3):
                r.rgbp[c, pl.ds(j, 1), :] = part[c : c + 1]
            tiles.append(tile)
            grads.append((grad * scale).astype(bf16))
        r.dq_sum[...] += nt(side(tiles), side(grads))

    middle_tile = head + (tail - head) // 2 // BIG_UNROLL * BIG_UNROLL
    loop(0, head, partial(backward, True), HEAD_UNROLL)
    loop(head, middle_tile, partial(backward, False), BIG_UNROLL)
    if fused:
        pack_rows = PACK // parts
        mine = pl.ds(pl.multiple_of(place * pack_rows, 16), pack_rows)
        wait(quad_pack)
        r.pack_m[...] = summed(r.pack_c[quad], r.pack_q).astype(bf16)
        z_pack = send_z(
            lambda to: r.pack_m.at[pl.ds(pl.multiple_of(to * pack_rows, 16), pack_rows)], lambda s: r.pack_z.at[s - 1]
        )
        first_down.wait()
        for b in range(2):
            r.down_1[b] = r.down_1[b] + r.down_c[x * 2 + b]
        second_down = send(r.down_1.at[1 - y], r.down_2, away(2)[1])
    loop(middle_tile, tail, partial(backward, False), BIG_UNROLL)
    if fused:
        wait(z_pack)
        r.pack_own[...] = summed(r.pack_m[mine, :], r.pack_z).astype(bf16)
        r.pack_all[core, quad, mine, :] = r.pack_own[...]
        all_pack = send_z(lambda to: r.pack_own, lambda s: r.pack_all.at[core, quad, mine])
    loop(tail, last, partial(backward, True), HEAD_UNROLL)

    dq = r.dq_sum[...].T
    lanes = lax.broadcasted_iota(jnp.int32, dq.shape, 1)
    gs_sum = dq[:, FEAT : FEAT + 1] + dq[:, FEAT + 1 : FEAT + 2]
    dq = jnp.where(lanes == FEAT, gs_sum, centred(dq, 1)).astype(bf16)
    r.dq_pay[...] = jnp.zeros_like(r.dq_pay)
    each = own // 8
    for d in range(8):
        r.dq_pay[d % 2, d // 2, :, :WIDE] = dq[d * each : (d + 1) * each]
    if fused:
        core_dq = send(r.dq_pay.at[1 - core], r.dq_c, mate)

    for t in range(parts):
        r.rgb_send[t] = jnp.concatenate(
            [r.rgbp[c, t * per : (t + 1) * per, :] for c in range(3)] + [jnp.zeros((per, TILE), f32)], axis=0
        ).astype(bf16)
    back_copies = send_z(lambda to: r.rgb_send.at[to], lambda s: r.rgb_back.at[s - 1])

    if fused:
        core_dq.wait()
        r.dq_c[...] = r.dq_c[...] + r.dq_pay[core]
        quad_dq = send_quad(lambda q: r.dq_c.at[q], lambda k: r.dq_q.at[k - 1])
        wait(out_copies)
        unit, scale = norm(r.latents[...].astype(f32))
        r.mid_unit[...] = unit
        r.mid_scale[...] = scale
        lat_low = (unit * r.vecs[2:3, :] + r.vecs[3:4, :]).astype(bf16)
        r.cot_send[...] = lat_low.reshape(parts, own, width)
        queries = ((nn(lat_low, r.wq[...]) + r.vecs[0:1, :]) * factor).astype(bf16)
        r.out_send[...] = queries.reshape(parts, own, width)
        r.qk_all[...] = nt(queries, r.wk[...])
        wait(all_pack)
        all_pack = send_quad(lambda q: r.pack_all.at[core, quad], lambda k: r.pack_all.at[core, quad])
        first_up.wait()
        for b in range(2):
            r.up_1[b] = r.up_1[b] + r.up_c[y * 2 + b]
        second_up = send(r.up_1.at[1 - x], r.up_2, away(1)[1])
        wait(quad_dq)
        r.dq_own[...] = summed(r.dq_c[quad], r.dq_q).astype(bf16)
        r.dq_all[core, quad, place] = r.dq_own[...]
        z_dq = send_z(lambda to: r.dq_own, lambda s: r.dq_all.at[core, quad, place])
        second_down.wait()
        r.down_m[...] = (r.down_1[y].astype(f32) + r.down_2[...].astype(f32)).astype(bf16)
        z_down = send_z(
            lambda to: r.down_m.at[pl.ds(pl.multiple_of(to * chunk, 16), chunk)], lambda s: r.down_z.at[s - 1]
        )
        wait(z_dq)
        all_dq = send_quad(lambda q: r.dq_all.at[core, quad], lambda k: r.dq_all.at[core, quad])

    wait(back_copies)
    r.rgb_out[...] = summed(r.rgb_send[place], r.rgb_back).astype(bf16)

    if fused:
        wait(all_dq)
        all_dq = send(r.dq_all.at[core], r.dq_all.at[core], mate)
        wait(all_pack)
        all_pack = send(r.pack_all.at[core], r.pack_all.at[core], mate)
        second_up.wait()
        up_sum = r.up_1[x].astype(f32) + r.up_2[...].astype(f32)
        r.up_m[...] = up_sum[:width].astype(bf16)
        z_up = send_z(
            lambda to: r.up_m.at[pl.ds(pl.multiple_of(to * chunk, 16), chunk)], lambda s: r.up_z.at[s - 1]
        )
        all_dq.wait()

        for z in range(parts):
            for d in range(8):
                r.dq[(z * 8 + d) * each : (z * 8 + d + 1) * each, :] = r.dq_all[d % 2, d // 2, z]
        own_cols = pl.ds(pl.multiple_of(lax.rem(group, 8) * LANES, LANES), LANES)
        lat_cols = pl.ds(pl.multiple_of(place * chunk, LANES), chunk)
        units = r.dq[...].astype(f32)
        lean = units[:, FEAT : FEAT + 1]
        units = jnp.where(lax.broadcasted_iota(jnp.int32, units.shape, 1) < FEAT, units, 0.0)
        gain_sum = jnp.sum(r.qk_all[...] * units, axis=0, keepdims=True)
        bias_sum = jnp.sum(r.qk_all[...] * lean, axis=0, keepdims=True)
        dx = (units * r.feats[0:1, :] + lean * r.feats[1:2, :]).astype(bf16)
        order = order_of(264, DQ)
        r.key_out[...] = nn(nt(order, dx).astype(bf16), r.out_send[...].reshape(count, width))[:FEAT]
        gq = nn(dx, r.wk[...]) * factor
        gq_low = gq.astype(bf16)
        query_bias = jnp.sum(gq, axis=0, keepdims=True)
        grad_lat = nt(gq_low, r.wq[...])
        latent_gain = jnp.sum(grad_lat * r.mid_unit[...], axis=0, keepdims=True)
        latent_bias = jnp.sum(grad_lat, axis=0, keepdims=True)
        r.out_send[...] = gq_low.reshape(parts, own, width)
        r.query_out[...] = tn(
            r.cot_send[:, :, lat_cols].reshape(count, chunk), r.out_send[:, :, own_cols].reshape(count, LANES)
        )
        r.mid_unit[...] = norm_back(grad_lat * r.vecs[2:3, :], r.mid_unit[...], r.mid_scale[...])
        r.latents_out[...] = up_sum[width:] + r.mid_unit[rows, own_cols]

        all_pack.wait()
        for d in range(8):
            r.moment[:, d * LANES : (d + 1) * LANES] = r.pack_all[d % 2, d // 2]
        r.value_out[...] = nt(nn(order[:, :WIDE], r.moment[:WIDE, :]).astype(bf16), r.wo[...])[:FEAT]
        r.out_out[...] = tn(r.wv[:, lat_cols], r.moment[:WIDE, own_cols])
        small = r.moment[WIDE : WIDE + 16, :]
        value_bias = nt(small, r.wo[...])[2:3]
        small = small.astype(f32)
        r.vec_out[...] = jnp.concatenate(
            [small[:8], value_bias, query_bias, latent_gain, latent_bias, jnp.zeros((4, width), f32)], axis=0
        )
        ends_of = jnp.concatenate(
            [small[5:6, :DQ] + gain_sum, small[6:7, :DQ] + bias_sum, jnp.zeros((6, DQ), f32)], axis=0
        )
        r.ext_out[...] = moved(ends_of, order_of(DQ, DQ), nt)

        block = pl.ds(pl.multiple_of(place * chunk, 16), chunk)
        wait(z_down)
        r.down_out[...] = summed(r.down_m[block, :], r.down_z)
        wait(z_up)
        r.up_out[...] = summed(r.up_m[block, :], r.up_z)
    else:
        wait(out_copies)


def layer(images, slots, parts, fused, sizes, rgb, latents, wq, wo, up, down, wk, wv, cot, vecs):
    count, width = latents.shape
    own, chunk = count // parts, width // parts
    rows = images * own
    hidden = up.shape[1]
    tiles = slots // TILE
    last = tiles_of(images, slots)[2]
    each = own // 8
    any_, vm = pl.BlockSpec(memory_space=pl.ANY), pl.BlockSpec(memory_space=pltpu.VMEM)
    sds = jax.ShapeDtypeStruct
    V = pltpu.VMEM
    ins = [
        ("sizes", sizes, pl.BlockSpec(memory_space=pltpu.SMEM)), ("rgb_in", rgb, vm), ("latents", latents, vm),
        ("wq_h", wq, any_), ("wo_h", wo, any_), ("up_h", up, any_), ("down_h", down, any_),
        ("wk_in", wk, vm), ("wv_in", wv, vm), ("cot_h", cot, any_), ("vecs", vecs, vm),
    ]
    pays = [
        ("down_pay", (2, 4, hidden, LANES), bf16), ("up_pay", (2, 4, width + own, LANES), bf16),
        ("pack", (2, 4, PACK, LANES), bf16), ("dq_pay", (2, 4, each, DQ), bf16),
        ("wk", (DQ, width), bf16), ("wv", (WIDE, width), bf16), ("feats", (8, DQ), f32),
    ]
    outs = [("out_rows", (parts, own, width), bf16), ("rgb_out", rgb.shape, bf16)]
    scratch = [
        ("feat", (last, WIDE, TILE), bf16), ("stat", (last, 8, TILE), f32), ("wst", (last, own, TILE), bf16),
        ("rgb_recv", (parts - 1,) + rgb.shape, bf16), ("rgbf", (3, tiles, TILE), f32), ("rgbp", (3, tiles, TILE), f32),
        ("rgb_send", (parts,) + rgb.shape, bf16), ("rgb_back", (parts - 1,) + rgb.shape, bf16),
        ("wq", wq.shape, bf16), ("wo", wo.shape, bf16), ("up", up.shape, bf16), ("down", down.shape, bf16),
        ("cot_f", cot.shape, f32), ("cot_send", (parts, own, width), bf16), ("cot_low", (parts, own, width), bf16),
        ("out_send", (parts, own, width), bf16),
        ("qc", (own, WIDE), bf16), ("qb", (own, 1), f32), ("ext", (images * 16 + 16, own), bf16),
        ("extb", (16, 2 * own), bf16),
        ("acc", (WIDE, rows), f32), ("acc_big", (WIDE, own), f32), ("unit", (rows, WIDE), f32), ("px", (rows, WIDE), bf16),
        ("wvo", (WIDE, width), bf16), ("tot", (rows, 1), f32),
        ("mid_unit", (rows, width), f32), ("mid_scale", (rows, 1), f32),
        ("act_t", (hidden, rows), bf16), ("mid_t", (width, rows), bf16), ("px_t", (WIDE, rows), bf16),
        ("gh", (rows, hidden), bf16), ("branch", (rows, width), bf16), ("gx", (rows, WIDE), f32),
        ("gc", (rows, WIDE), bf16), ("gcb", (own, WIDE), bf16), ("lev", (rows, 1), f32), ("levb", (own, 1), f32),
        ("dq_sum", (WIDE, own), f32),
    ]
    if fused:
        outs += [
            ("down_out", (chunk, LANES), f32), ("up_out", (chunk, LANES), f32), ("out_out", (chunk, LANES), f32),
            ("query_out", (chunk, LANES), f32), ("latents_out", (own, LANES), f32), ("key_out", (FEAT, width), f32),
            ("value_out", (FEAT, width), f32), ("vec_out", (16, width), f32), ("ext_out", (8, DQ), f32),
        ]
        tall = width + own
        scratch += pays + [
            ("down_c", (4, hidden, LANES), bf16), ("down_1", (2, hidden, LANES), bf16), ("down_2", (hidden, LANES), bf16),
            ("down_m", (hidden, LANES), bf16), ("down_z", (parts - 1, chunk, LANES), bf16),
            ("up_c", (4, tall, LANES), bf16), ("up_1", (2, tall, LANES), bf16), ("up_2", (tall, LANES), bf16),
            ("up_m", (width, LANES), bf16), ("up_z", (parts - 1, chunk, LANES), bf16),
            ("pack_c", (4, PACK, LANES), bf16), ("pack_q", (3, PACK, LANES), bf16), ("pack_m", (PACK, LANES), bf16),
            ("pack_z", (parts - 1, PACK // parts, LANES), bf16), ("pack_own", (PACK // parts, LANES), bf16),
            ("pack_all", (2, 4, PACK, LANES), bf16),
            ("dq_c", (4, each, DQ), bf16), ("dq_q", (3, each, DQ), bf16), ("dq_own", (each, DQ), bf16),
            ("dq_all", (2, 4, parts, each, DQ), bf16), ("dq", (count, DQ), bf16), ("moment", (PACK, width), bf16),
            ("qk_all", (count, DQ), f32),
        ]
    else:
        outs += pays
    names = [n for n, _, _ in ins + outs + scratch] + ["load_sems", "sems"]
    return pl.pallas_call(
        partial(layer_kernel, images, slots, parts, fused, names),
        out_shape=tuple(sds(s, d) for _, s, d in outs),
        in_specs=[spec for _, _, spec in ins],
        out_specs=(vm,) * len(outs),
        scratch_shapes=[V(s, d) for _, s, d in scratch]
        + [pltpu.SemaphoreType.DMA((5,)), pltpu.SemaphoreType.DMA((2, SENDS))],
        compiler_params=pltpu.CompilerParams(collective_id=0, has_side_effects=True, vmem_limit_bytes=VMEM_LIMIT),
        name="layer",
    )(*[a for _, a, _ in ins])


def finish_kernel(moves, *refs):
    rows, rgb, vec, ext = refs[:4]
    whole = refs[4 : 4 + moves]
    lat_out, rgb_grad = refs[4 + moves : 6 + moves]
    whole_out = refs[6 + moves : 6 + 2 * moves]
    vec_out = refs[6 + 2 * moves : -1]
    sems = refs[-1]
    copies = [pltpu.make_async_copy(a, b, sems.at[i]) for i, (a, b) in enumerate(zip(whole, whole_out))]
    for copy in copies:
        copy.start()
    parts, own, width = rows.shape
    lat_out[0] = rows[...].reshape(parts * own, width).astype(f32)
    colours = rgb[...].astype(f32)
    per = rgb.shape[0] // 4
    rgb_grad[...] = jnp.concatenate(
        [
            jnp.concatenate([colours[c * per + j : c * per + j + 1] for j in range(per)], axis=1)
            for c in range(3)
        ],
        axis=0,
    ).astype(bf16)
    for i, out in enumerate(vec_out[:9]):
        out[...] = vec[i if i < 5 else i + 3, :]
    for i, out in enumerate(vec_out[9:]):
        out[...] = ext[i, :FEAT]
    wait(copies)


def finish(rows, rgb, vec, ext, *whole):
    parts, own, width = rows.shape
    any_, vm = pl.BlockSpec(memory_space=pl.ANY), pl.BlockSpec(memory_space=pltpu.VMEM)
    sds = jax.ShapeDtypeStruct
    n = len(whole)
    return pl.pallas_call(
        partial(finish_kernel, n),
        out_shape=(sds((1, parts * own, width), f32), sds((3, rgb.shape[0] // 4 * TILE), bf16))
        + tuple(sds(a.shape, a.dtype) for a in whole)
        + (sds((width,), f32),) * 9
        + (sds((FEAT,), f32),) * 2,
        in_specs=[vm] * 4 + [any_] * n,
        out_specs=(vm,) * 2 + (any_,) * n + (vm,) * 11,
        scratch_shapes=[pltpu.SemaphoreType.DMA((n,))],
        compiler_params=pltpu.CompilerParams(vmem_limit_bytes=32 * 2**20),
        name="finish",
    )(rows, rgb, vec, ext, *whole)


def restore(rows):
    b = 2 * BANDS
    return jnp.concatenate(
        [rows[2 * b : 2 * b + 4], rows[:b], rows[2 * b + 4 : 2 * b + 5], rows[b : 2 * b]], axis=0
    )


def sums_plain(parts, down_pay, up_pay, pack, dq, latents, wq, wo, wk, wv, vecs, feats):
    count, width = latents.shape
    own, chunk = count // parts, width // parts
    place, group, groups = lax.axis_index("pix"), lax.axis_index("dp"), lax.axis_size("dp")
    cols = width // groups
    factor = 1.0 / math.sqrt(width)

    def flat(a):
        return a.transpose(2, 1, 0, 3).reshape(a.shape[2], width).astype(f32)

    down_pay = down_pay.reshape(2, 2, 2, *down_pay.shape[2:]).transpose(0, 2, 1, 3, 4).reshape(down_pay.shape)

    def scattered(a):
        a = lax.psum_scatter(a, "dp", scatter_dimension=1, tiled=True)
        return lax.psum_scatter(a, "pix", scatter_dimension=0, tiled=True)

    up_all = flat(up_pay)
    down_total, up_total = scattered(flat(down_pay)), scattered(up_all[:width])
    latents_sum = lax.psum_scatter(up_all[width:], "dp", scatter_dimension=1, tiled=True)
    moment = lax.psum(flat(pack), ("dp", "pix"))
    small, moment = moment[WIDE : WIDE + 8], moment[:WIDE].astype(bf16)
    units = lax.psum(dq.transpose(1, 0, 2, 3).reshape(own, DQ).astype(f32), "dp")
    units = lax.all_gather(units, "pix", axis=0, tiled=True)

    unit, scale = norm(latents.astype(f32))
    lat_in = (unit * vecs[2] + vecs[3]).astype(bf16)
    queries = ((nn(lat_in, wq) + vecs[0]) * factor).astype(bf16)
    lean = units[:, FEAT : FEAT + 1]
    units = units * (jnp.arange(DQ) < FEAT)
    qk = nt(queries, wk)
    ext = jnp.zeros((8, DQ), f32)
    ext = ext.at[0].set(small[5, :DQ] + jnp.sum(qk * units, axis=0))
    ext = ext.at[1].set(small[6, :DQ] + jnp.sum(qk * lean, axis=0))
    dx = (units * feats[0] + lean * feats[1]).astype(bf16)
    key_total = restore(tn(dx, queries))
    gq = nn(dx, wk) * factor
    gq_low = gq.astype(bf16)
    grad_lat = nt(gq_low, wq)
    own_cols = lambda a: lax.dynamic_slice_in_dim(a, group * cols, cols, axis=1)
    own_rows = lambda a: lax.dynamic_slice_in_dim(a, place * chunk, chunk, axis=1)
    query_total = tn(own_rows(lat_in), own_cols(gq_low))
    back = norm_back(grad_lat * vecs[2], unit, scale)
    latents_total = latents_sum + own_cols(lax.dynamic_slice_in_dim(back, place * own, own, axis=0))
    value_total = restore(nt(moment, wo))
    out_total = tn(own_rows(wv), own_cols(moment))
    vec = jnp.concatenate(
        [
            small,
            nt(small.astype(bf16), wo)[2:3],
            jnp.sum(gq, axis=0, keepdims=True),
            jnp.sum(grad_lat * unit, axis=0, keepdims=True),
            jnp.sum(grad_lat, axis=0, keepdims=True),
        ],
        axis=0,
    )
    return down_total, up_total, out_total, query_total, latents_total, key_total, value_total, vec, ext

def shards(
    latents,
    pixel_rgb,
    coords,
    segment_ids,
    image_sizes,
    input_gain,
    input_bias,
    query_weight,
    query_bias,
    key_weight,
    value_weight,
    value_bias,
    out_weight,
    out_bias,
    latent_gain,
    latent_bias,
    mlp_gain,
    mlp_bias,
    up_weight,
    up_bias,
    down_weight,
    down_bias,
    cotangent,
):
    images = image_sizes.shape[1]
    width = latents.shape[1]
    parts = lax.axis_size("pix")
    slots = pixel_rgb.shape[1] * parts
    tiles = pixel_rgb.shape[1] // TILE
    rgb = jnp.pad(pixel_rgb.reshape(3, tiles, TILE), ((0, 1), (0, 0), (0, 0))).reshape(4 * tiles, TILE)
    fill = lambda v: jnp.pad(v, (0, width - FEAT))
    none = jnp.zeros((width,), f32)
    vecs = jnp.stack(
        [
            query_bias, out_bias, latent_gain, latent_bias, mlp_gain, mlp_bias, up_bias, down_bias,
            fill(input_gain), fill(input_bias), value_bias, none, none, none, none, none,
        ],
        axis=0,
    )
    fused = lax.axis_size("dp") == 8
    rows, rgb_out, *rest = layer(
        images, slots, parts, fused, image_sizes, rgb, latents, query_weight, out_weight, up_weight, down_weight,
        key_weight, value_weight, cotangent, vecs,
    )
    if fused:
        down, up, out, query, latents_sum, key, value, vec, ext = rest
        (
            latents_out, rgb_grad, down, up, out, query, latents_sum, key, value,
            db, ub, ob, mg, mb, vb, qb, lg, lb, gain, bias,
        ) = finish(rows, rgb_out, vec, ext, down, up, out, query, latents_sum, key, value)
    else:
        down, up, out, query, latents_sum, key, value, vec, ext = sums_plain(
            parts, *rest[:4], latents, query_weight, out_weight, rest[4], rest[5], vecs, rest[6]
        )
        latents_out = rows.reshape(1, latents.shape[0], width).astype(f32)
        rgb_grad = rgb_out.reshape(4, tiles, TILE)[:3].reshape(3, tiles * TILE)
        db, ub, ob, mg, mb = (vec[i] for i in range(5))
        vb, qb, lg, lb = (vec[i] for i in range(8, 12))
        gain, bias = restore(ext[0]), restore(ext[1])
    return (
        latents_out, rgb_grad, latents_sum, query, qb, key, value, vb, out, ob, lg, lb, mg, mb, up, ub, down, db,
        gain, bias,
    )


def solution(mesh):
    whole = P()
    placed = (
        whole,
        P(None, ("dp", "pix")),
        P(None, ("dp", "pix")),
        P(("dp", "pix")),
        P(None, "dp"),
    ) + (whole,) * 17 + (P(("dp", "pix"), None, None),)
    square = P("pix", "dp")
    return jax.shard_map(
        shards,
        mesh=mesh,
        in_specs=placed,
        out_specs=(
            P(("dp", "pix"), None, None),
            P(None, ("dp", "pix")),
            square,
            square,
            whole,
            whole,
            whole,
            whole,
            square,
            whole,
            whole,
            whole,
            whole,
            whole,
            square,
            whole,
            square,
            whole,
            whole,
            whole,
        ),
        check_vma=False,
    )
```

time: 672 us -> 124 us (0.18); the launches traced: 663 us -> 123 us
  waiting for transfers between devices: 229 us -> 0 us
  other arithmetic: 130 us -> 0 us
  matrix products: 120 us -> 0 us
  Pallas kernels: 0 us -> 106 us
  blocking collectives: 86.6 us -> 0 us
  local copies, waits for them, and re-layouts: 65.5 us -> 16 us
  between operations: 20.6 us -> 0.87 us
  starting transfers between devices: 11.4 us -> 0 us
    unnamed x8 -> x0, waiting for transfers between devices: 141 us -> none
    dot_general x33 -> x0, matrix products: 120 us -> none  [dot(): return lax.dot_general(a, b, (dims, ((), ())), preferred_element_type=f32)]
    pallas_call x0 -> x2, Pallas kernels: none -> 106 us  [the longest x1 103 us: layer(): pl.pallas_call(partial(layer_kernel, images, slots, parts, fused, names),...]
    reduce_scatter x5 -> x0, waiting for transfers between devices: 87.6 us -> none  [the longest x1 34.9 us: shards(): lax.psum_scatter(latents_part, 'dp', scatter_dimension=1, tiled=True)]
    psum x1 -> x0, blocking collectives: 56.1 us -> none  [shards(): lax.psum((moment, out_bias_grad, up_bias_grad, down_bias_grad, mlp_gain_g...]
    another operation x2 -> x0, other arithmetic: 44.1 us -> none
    concatenate x1 -> x0, local copies, waits for them, and re-layouts: 39.5 us -> none  [pixel_features(): jnp.concatenate([jnp.sin(py), jnp.cos(py), jnp.sin(px), jnp.cos(px), rest...]
    convert_element_type x9 -> x0, other arithmetic: 33.4 us -> none  [the longest x1 12.5 us: shards(): ((weights * scale)[None] * member[:, None]).astype(bf16)]
  transfers between devices with their start and end apart: 9 -> 0, of which waited for: 5 -> 0; matrix products, arithmetic and copies ran while one was open for 37% -> 0% of each run, Pallas kernels for 0% -> 0%
where the time goes in v2:
time: 124 us; the launch traced here: 123 us
  Pallas kernels  106 us (85%)
  local copies, waits for them, and re-layouts  16 us (13%)
    pallas_call x1, Pallas kernels, layer(): pl.pallas_call(partial(layer_kernel, images, slots, parts, fused, names),...  103 us
    unnamed x23, local copies, waits for them, and re-layouts  11.2 us
    pallas_call x1, Pallas kernels, finish(): pl.pallas_call(partial(finish_kernel, n), out_shape=(sds((1, parts * own,...  2.95 us
    another operation x3, local copies, waits for them, and re-layouts, shards(): jnp.stack([query_bias, out_bias, latent_gain, latent_bias, mlp_gain, mlp_...  2.8 us

profile of v2, /device:TPU:0, one launch (start us, length us, event | category | flops | bytes accessed | tf_op | source)
XLA Modules:
  0.0 123.2 jit_solution(13633786649370409765)
XLA Ops:
  0.7 0.7 pad.12
  1.3 0.7 pad.13
  2.0 0.8 copy.43
  2.8 0.6 pad_bitcast_fusion.refs_1_
  3.4 2.8 %stack.51.refs_10_ = f32[16,1024]{1,0:T(8,128)} concatenate(f32[1,1024]{1,0:T(1,128)} %bitcast.21, f32[1,1024]{1,0:T(1,128)} %bitcast.22, f32[1,1024]{1,0:T(1,128)} %bitcast.23, f32[1,1024]{1,0:T(1,128)} %bitcast.24, f32[1,1024]{1,0:T(1,128)} %bitcast.25, f32[1,1024]{1,0:T(1,128)} %bitcast.26, f32[1,1024]{1,0:T(1,128)} %bitcast.27, f32[1,1024]{1,0:T(1,128)} %bitcast.28, ...), dimensions={0} | concatenate | bytes 131072 | tf_op jit(solution)/shard_map/stack | solution.py:870
  6.2 103.4 %layer.1 = (bf16[4,128,1024]{2,1,0:T(8,128)(2,1)}, bf16[32,512]{1,0:T(8,128)(2,1)}, f32[256,128]{1,0:T(8,128)}, f32[256,128]{1,0:T(8,128)}, f32[256,128]{1,0:T(8...) custom-call(s32[2,4]{1,0:T(2,128)} %refs_0_.1, ...), custom_call_target="tpu_custom_call" | custom-call | tf_op jit(solution)/shard_map/layer/pallas_call | solution.py:714
  109.6 0.0 copy-start
  109.6 1.2 copy-done
  110.9 0.0 copy-start.1
  110.9 1.2 %copy-done.1 = f32[261,1024]{1,0:T(8,128)S(1)} copy-done((f32[261,1024]{1,0:T(8,128)S(1)}, f32[261,1024]{1,0:T(8,128)}, u32[]{:S(2)}) %copy-start.1) | copy-done | bytes 1069080
  112.1 0.0 copy-start.2
  112.1 1.2 copy-done.2
  113.3 0.0 copy-start.3
  113.3 0.9 copy-done.3
  114.2 0.0 copy-start.4
  114.2 0.9 copy-done.4
  115.1 0.0 copy-start.5
  115.1 0.9 copy-done.5
  116.0 0.0 copy-start.6
  116.0 0.9 copy-done.6
  116.9 0.0 copy-start.7
  116.9 0.8 copy-done.7
  117.8 0.0 copy-start.8
  117.8 0.8 copy-done.8
  118.6 0.0 copy-start.9
  118.6 0.8 copy-done.9
  119.4 0.0 copy-start.10
  119.4 0.7 copy-done.10
  120.1 3.0 %finish.1 = (f32[1,512,1024]{2,1,0:T(8,128)}, bf16[3,4096]{1,0:T(4,128)(2,1)}, f32[256,128]{1,0:T(8,128)}, f32[256,128]{1,0:T(8,128)}, f32[256,128]{1,0:T(8,128)...) custom-call(bf16[4,128,1024]{2,1,0:T(8,128)(2,1)S(1)} %copy-done.2, ...), custom_call_target="tpu_custom_call" | custom-call | tf_op jit(solution)/shard_map/finish/pallas_call | solution.py:759
  (2 shorter events, 0.0 us)
Async XLA Ops:
  109.6 1.2 %copy-start = (f32[261,1024]{1,0:T(8,128)S(1)}, f32[261,1024]{1,0:T(8,128)}, u32[]{:S(2)}) copy-start(f32[261,1024]{1,0:T(8,128)} %get-tuple-element.60.refs_9_) | copy-start | bytes 3207172
  110.9 1.2 %copy-start.1 = (f32[261,1024]{1,0:T(8,128)S(1)}, f32[261,1024]{1,0:T(8,128)}, u32[]{:S(2)}) copy-start(f32[261,1024]{1,0:T(8,128)} %get-tuple-element.61.refs_10_) | copy-start | bytes 3207172
  112.1 1.2 copy-start.2
  113.3 0.9 copy-start.3
  114.2 0.9 copy-start.4
  115.1 0.9 copy-start.5
  116.0 0.9 copy-start.6
  116.9 0.8 copy-start.7
  117.8 0.8 copy-start.8
  118.6 0.8 copy-start.9
  119.4 0.7 copy-start.10

commit v3 on v2

--- a/solution.py
+++ b/solution.py
@@ -21,7 +21,7 @@
 TILE = 512
 LANES = 128
 MESH = pl.DeviceIdType.MESH
-SENDS = 49
+SENDS = 55
 VMEM_LIMIT = 62 * 2**20
 
 bf16 = jnp.bfloat16
@@ -134,7 +134,7 @@
 def layer_kernel(images, slots, parts, fused, names, *refs):
     r = SimpleNamespace(**dict(zip(names, refs)))
     group, place = lax.axis_index("dp"), lax.axis_index("pix")
-    count, width = r.latents.shape
+    count, width = r.latents_h.shape
     own, chunk = count // parts, width // parts
     rows_all = images * own
     head, tail, last = tiles_of(images, slots)
@@ -168,42 +168,44 @@
     def send_quad(pick, put):
         return [send(pick(away(k)[0]), put(k), away(k)[1]) for k in (1, 2, 3)]
 
+    barrier = pltpu.get_barrier_semaphore()
+    friends = [(group, to) for _, to, _ in zs]
+    if fused:
+        friends += [mate] + [away(k)[1] for k in (1, 2, 3)]
+    for device in friends:
+        pl.semaphore_signal(barrier, inc=1, device_id=device, device_id_type=MESH)
     loads = [
         pltpu.make_async_copy(a, b, r.load_sems.at[i])
         for i, (a, b) in enumerate(
-            ((r.cot_h, r.cot_f), (r.wq_h, r.wq), (r.wo_h, r.wo), (r.up_h, r.up), (r.down_h, r.down))
+            (
+                (r.wq_h, r.wq), (r.wo_h, r.wo), (r.cot_h, r.cot_f), (r.up_h, r.up), (r.down_h, r.down),
+                (r.latents_h, r.latents), (r.wv_h, r.wv_in),
+            )
         )
     ]
-    for copy in loads:
-        copy.start()
-
-    barrier = pltpu.get_barrier_semaphore()
-    friends = [(group, to) for _, to, _ in zs]
-    if fused:
-        friends += [mate] + [away(k)[1] for k in (1, 2, 3)]
-    for device in friends:
-        pl.semaphore_signal(barrier, inc=1, device_id=device, device_id_type=MESH)
-    pl.semaphore_wait(barrier, len(friends))
-
-    rgb_copies = send_z(lambda to: r.rgb_in, lambda s: r.rgb_recv.at[s - 1])
-    loads[0].wait()
-    r.cot_send[...] = r.cot_f[0].astype(bf16).reshape(parts, own, width)
-    cot_copies = send_z(lambda to: r.cot_send.at[to], lambda s: r.cot_low.at[place])
-    r.cot_low[place] = r.cot_send[place]
+    for i in (5, 0, 6, 1, 2, 3, 4):
+        loads[i].start()
+
+    shades = r.pixel_rgb[...].astype(f32)
+    pieces = [shades[c : c + 1, j * TILE : (j + 1) * TILE] for c in range(3) for j in range(per)]
+    r.rgb_in[...] = jnp.concatenate(pieces + [jnp.zeros((per, TILE), f32)], axis=0).astype(bf16)
+    r.vecs[...] = jnp.zeros_like(r.vecs)
+    for i in range(11):
+        vec = getattr(r, f"vec{i}")
+        r.vecs[i : i + 1, : vec.shape[0]] = vec[...].reshape(1, vec.shape[0])
 
     to_waves = order_of(WIDE, FEAT, flip=True)
     r.wk[:WIDE] = nn(to_waves, r.wk_in[...]).astype(bf16)
     r.wk[WIDE:] = jnp.zeros_like(r.wk[WIDE:])
-    vb = r.vecs[10:11, :]
-    vb_high = vb.astype(bf16).astype(f32)
-    row = lax.broadcasted_iota(jnp.int32, (WIDE, width), 0)
-    wv = nn(to_waves, r.wv_in[...])
-    r.wv[...] = jnp.where(row == FEAT, vb_high, jnp.where(row == FEAT + 1, vb - vb_high, wv)).astype(bf16)
     feats = moved(r.vecs[8:16, :DQ], order_of(DQ, DQ), nn)
     r.feats[...] = feats
     gain, bias = feats[0:1, :WIDE], feats[1:2, :WIDE]
 
-    loads[1].wait()
+    pl.semaphore_wait(barrier, len(friends))
+    rgb_copies = send_z(lambda to: r.rgb_in, lambda s: r.rgb_recv.at[s - 1])
+
+    loads[5].wait()
+    loads[0].wait()
     rows = pl.ds(pl.multiple_of(place * own, own), own)
     lat_rows = r.latents[rows, :].astype(f32)
     own_unit, _ = norm(lat_rows)
@@ -218,6 +220,13 @@
         == lax.broadcasted_iota(jnp.int32, (16, WIDE), 0) + 4 * BANDS
     ).astype(bf16)
     r.ext[images * 16 :, :] = nt(pick, qc).astype(bf16)
+
+    loads[6].wait()
+    vb = r.vecs[10:11, :]
+    vb_high = vb.astype(bf16).astype(f32)
+    row = lax.broadcasted_iota(jnp.int32, (WIDE, width), 0)
+    wv = nn(to_waves, r.wv_in[...])
+    r.wv[...] = jnp.where(row == FEAT, vb_high, jnp.where(row == FEAT + 1, vb - vb_high, wv)).astype(bf16)
 
     wait(rgb_copies)
     for c in range(3):
@@ -320,10 +329,6 @@
     loop(head, tail, partial(forward, False), BIG_UNROLL)
     loop(tail, last, partial(forward, True), HEAD_UNROLL)
 
-    loads[2].wait()
-    wvo = nn(r.wv[...], r.wo[...])
-    const = wvo[FEAT : FEAT + 1] + wvo[FEAT + 1 : FEAT + 2] + r.vecs[1:2, :]
-    r.wvo[...] = jnp.where(row < FEAT, wvo, 0.0).astype(bf16)
     lane = lax.broadcasted_iota(jnp.int32, (own, WIDE), 1)
     ones = ((lane == FEAT) | (lane == FEAT + 1)).astype(f32)
     big = r.acc_big[...]
@@ -335,42 +340,47 @@
         unit = centred(mix, 1) / totals
         r.tot[at, :] = totals
         r.unit[at, :] = unit
-        r.px[at, :] = (unit * gain + bias + ones).astype(bf16)
-
+        r.px_send[n] = (unit * gain + bias + ones).astype(bf16).T
+    px_copies = send_z(lambda to: r.px_send.at[to], lambda s: r.px_recv.at[place])
+    r.px_recv[place] = r.px_send[place]
+
+    loads[1].wait()
+    wvo = nn(r.wv[...], r.wo[...])
+    const = wvo[FEAT : FEAT + 1] + wvo[FEAT + 1 : FEAT + 2] + r.vecs[1:2, :]
+    r.wvo[...] = jnp.where(row < FEAT, wvo, 0.0).astype(bf16)
+    loads[2].wait()
     loads[3].wait()
     loads[4].wait()
     k = math.sqrt(2.0 / math.pi)
     half = 2 * own
+    wait(px_copies)
     out_copies = []
-    for blk in range(rows_all // half):
+    for blk in range(count // half):
         at = slice(blk * half, (blk + 1) * half)
-        px = r.px[at, :]
-        middle = jnp.concatenate([lat_rows] * (half // own), axis=0) + nn(px, r.wvo[...]) + const
+        px_t = jnp.concatenate([r.px_recv[2 * blk + i] for i in range(2)], axis=1)
+        r.px_t[:, at] = px_t
+        middle = r.latents[at, :].astype(f32) + nn(px_t.T, r.wvo[...]) + const
         mid_unit, mid_scale = norm(middle)
         mid_in = (mid_unit * r.vecs[4:5, :] + r.vecs[5:6, :]).astype(bf16)
         hidden = nn(mid_in, r.up[...]) + r.vecs[6:7, :]
         th = tanh(k * (hidden + 0.044715 * hidden * hidden * hidden))
         active = (0.5 * hidden * (1.0 + th)).astype(bf16)
-        r.cot_f[0, at, :] = 0.5 * (1.0 + th) + 0.5 * hidden * (1.0 - th * th) * k * (
+        r.slope[at, :] = 0.5 * (1.0 + th) + 0.5 * hidden * (1.0 - th * th) * k * (
             1.0 + 3 * 0.044715 * hidden * hidden
         )
-        done = (middle + nn(active, r.down[...]) + r.vecs[7:8, :]).astype(bf16)
-        r.out_send[2 * blk] = done[:own]
-        r.out_send[2 * blk + 1] = done[own:]
+        stage = (r.key_out, r.value_out)[blk].at[pl.ds(0, half)] if fused else (r.stage0, r.stage1)[blk]
+        stage[...] = middle + nn(active, r.down[...]) + r.vecs[7:8, :]
+        copy = pltpu.make_async_copy(stage, r.out_rows.at[0, pl.ds(blk * half, half)], r.load_sems.at[7 + blk])
+        copy.start()
+        out_copies.append(copy)
         r.mid_unit[at, :] = mid_unit
         r.mid_scale[at, :] = mid_scale
         r.act_t[:, at] = active.T
         r.mid_t[:, at] = mid_in.T
-        r.px_t[:, at] = px.T
-    out_copies = send_z(lambda to: r.out_send.at[to], lambda s: r.out_rows.at[place])
-    r.out_rows[place] = r.out_send[place]
-
-    wait(cot_copies)
 
     def down_grads(jj, c):
         cols = pl.ds(pl.multiple_of(jj * 256, 256), 256)
-        grads = jnp.concatenate([r.cot_low[n, :, cols] for n in range(images)], axis=0)
-        part = nn(r.act_t[...], grads).astype(bf16)
+        part = nn(r.act_t[...], r.cot_f[0, :, cols].astype(bf16)).astype(bf16)
         for i in range(2):
             r.down_pay[i, lax.rem(jj, 2) * 2 + jj // 2] = part[:, i * LANES : (i + 1) * LANES]
         return c
@@ -379,40 +389,52 @@
     if fused:
         core_down = send(r.down_pay.at[1 - core], r.down_c, mate)
 
-    total_sums, lat_sum, ext_total = None, None, None
-    for blk in range(rows_all // half):
+    def fold(first, value):
+        for i in range(width // count):
+            r.act_t[i * count + first : i * count + first + value.shape[0], :] = value[:, i * count : (i + 1) * count]
+
+    def unfold(first, size):
+        at = pl.ds(pl.multiple_of(first // count * count, count), count)
+        return r.act_t[at, pl.ds(pl.multiple_of(lax.rem(first, count), LANES), size)]
+
+    total_sums, ext_total = None, None
+    for blk in range(count // half):
         at = slice(blk * half, (blk + 1) * half)
-        grad_down = r.cot_low[2 * blk : 2 * blk + 2].reshape(half, width)
-        grad_hidden = (r.cot_f[0, at, :] * nt(grad_down, r.down[...])).astype(bf16)
-        r.gh[at, :] = grad_hidden
+        grad_down = r.cot_f[0, at, :].astype(bf16)
+        grad_hidden = (r.slope[at, :] * nt(grad_down, r.down[...])).astype(bf16)
+        fold(blk * half, grad_hidden)
         grad_mid = nt(grad_hidden, r.up[...])
         mid_unit = r.mid_unit[at, :]
-        cot = grad_down.astype(f32)
-        grad_middle = cot + norm_back(grad_mid * r.vecs[4:5, :], mid_unit, r.mid_scale[at, :])
+        grad_middle = r.cot_f[0, at, :] + norm_back(grad_mid * r.vecs[4:5, :], mid_unit, r.mid_scale[at, :])
         branch = grad_middle.astype(bf16)
         r.branch[at, :] = branch
+        for d in range(width // LANES):
+            q = d // 2
+            r.lat_pay[d % 2, q % 2 * 2 + q // 2, at, :] = branch[:, d * LANES : (d + 1) * LANES]
         part = [
             jnp.sum(v, axis=0, keepdims=True)
-            for v in (cot, grad_hidden.astype(f32), branch.astype(f32), grad_mid * mid_unit, grad_mid)
+            for v in (grad_down.astype(f32), grad_hidden.astype(f32), branch.astype(f32), grad_mid * mid_unit, grad_mid)
         ]
         total_sums = part if total_sums is None else [u + v for u, v in zip(total_sums, part)]
-        both = grad_middle[:own] + grad_middle[own:]
-        lat_sum = both if lat_sum is None else lat_sum + both
-        gx = nt(branch, r.wvo[...])
-        r.gx[at, :] = gx
-        part = [jnp.sum(gx * r.unit[at, :], axis=0, keepdims=True), jnp.sum(gx, axis=0, keepdims=True)]
+        gx = nt(r.wvo[...], branch)
+        r.px_send[2 * blk] = gx[:, :own].astype(bf16)
+        r.px_send[2 * blk + 1] = gx[:, own:].astype(bf16)
+        part = [jnp.sum(gx * r.px_t[:, at].astype(f32), axis=1, keepdims=True), jnp.sum(gx, axis=1, keepdims=True)]
         ext_total = part if ext_total is None else [u + v for u, v in zip(ext_total, part)]
+    gx_copies = send_z(lambda to: r.px_send.at[to], lambda s: r.gx_recv.at[place])
+    r.gx_recv[place] = r.px_send[place]
+    lane = lax.broadcasted_iota(jnp.int32, (WIDE, LANES), 1)
+    ext_rows = jnp.where(lane == 0, ext_total[0], jnp.where(lane == 1, ext_total[1], 0.0)).T
+    live = lax.broadcasted_iota(jnp.int32, (1, WIDE), 1) < FEAT
+    gain_part = jnp.where(live, (ext_rows[0:1] - bias * ext_rows[1:2]) / jnp.where(live, gain, 1.0), 0.0)
     small = jnp.concatenate(
         total_sums
-        + [jnp.pad(v, ((0, 0), (0, width - WIDE))) for v in ext_total]
+        + [jnp.pad(v, ((0, 0), (0, width - WIDE))) for v in (gain_part, jnp.where(live, ext_rows[1:2], 0.0))]
         + [jnp.zeros((PACK - WIDE - 7, width), f32)],
         axis=0,
     ).astype(bf16)
-    lat_low = lat_sum.astype(bf16)
     for d in range(width // LANES):
-        cols = slice(d * LANES, (d + 1) * LANES)
-        r.pack[d % 2, d // 2, WIDE:, :] = small[:, cols]
-        r.up_pay[d % 2, d // 2, width:, :] = lat_low[:, cols]
+        r.pack[d % 2, d // 2, WIDE:, :] = small[:, d * LANES : (d + 1) * LANES]
 
     if fused:
         core_down.wait()
@@ -429,23 +451,34 @@
 
     def up_grads(jj, c):
         cols = pl.ds(pl.multiple_of(jj * 256, 256), 256)
-        part = nn(r.mid_t[...], r.gh[:, cols]).astype(bf16)
+        part = nn(r.mid_t[...], unfold(jj * 256, 256)).astype(bf16)
         for i in range(2):
-            r.up_pay[i, jj, :width] = part[:, i * LANES : (i + 1) * LANES]
+            r.up_pay[i, jj] = part[:, i * LANES : (i + 1) * LANES]
         return c
 
     lax.fori_loop(0, width // 256, moments, 0)
     if fused:
         core_pack = send(r.pack.at[1 - core], r.pack_c, mate)
+        core_lat = send(r.lat_pay.at[1 - core], r.lat_c, mate)
     lax.fori_loop(0, width // 256, up_grads, 0)
     if fused:
         core_up = send(r.up_pay.at[1 - core], r.up_c, mate)
 
+    if fused:
+        unit, scale = norm(r.latents[...].astype(f32))
+        r.mid_unit[...] = unit
+        r.mid_scale[...] = scale
+        lat_low = (unit * r.vecs[2:3, :] + r.vecs[3:4, :]).astype(bf16)
+        fold(0, lat_low)
+        queries = ((nn(lat_low, r.wq[...]) + r.vecs[0:1, :]) * factor).astype(bf16)
+        r.branch[...] = queries
+        r.qk_all[...] = nt(queries, r.wk[...])
+    wait(gx_copies)
     gcb = jnp.zeros((own, WIDE), f32)
     levb = jnp.zeros((own, 1), f32)
     for n in range(images):
         at = slice(n * own, (n + 1) * own)
-        gc = centred(r.gx[at, :] / r.tot[at, :] * gain, 1)
+        gc = centred(r.gx_recv[n].T.astype(f32) * gain, 1) / r.tot[at, :]
         gc_low = gc.astype(bf16)
         level = jnp.sum(gc_low.astype(f32) * r.unit[at, :], axis=1, keepdims=True)
         r.gc[at, :] = gc_low
@@ -453,15 +486,21 @@
         r.ext[n * 16 : (n + 1) * 16, :] = nt(pick, gc_low).astype(bf16)
         gcb = gcb + gc * is_big[n]
         levb = levb + level * is_big[n]
-    r.gcb[...] = gcb.astype(bf16)
+    r.gc[rows_all :, :] = r.qc[...]
+    r.gcb[:own, :] = gcb.astype(bf16)
+    r.gcb[own:, :] = r.qc[...]
     r.levb[...] = levb
-    r.extb[:, own:] = nt(pick, r.gcb[...]).astype(bf16)
+    r.extb[:, own:] = nt(pick, r.gcb[:own, :]).astype(bf16)
     r.extb[:, :own] = r.ext[images * 16 :, :]
 
     if fused:
         core_pack.wait()
         r.pack_c[...] = r.pack_c[...] + r.pack[core]
         quad_pack = send_quad(lambda q: r.pack_c.at[q], lambda k: r.pack_q.at[k - 1])
+        core_lat.wait()
+        for b in range(4):
+            r.lat_c[b] = r.lat_c[b] + r.lat_pay[core, b]
+        first_lat = send(r.lat_c.at[pl.ds((1 - x) * 2, 2)], r.lat_1, away(1)[1])
         core_up.wait()
         for b in range(4):
             r.up_c[b] = r.up_c[b] + r.up_pay[core, b]
@@ -478,10 +517,10 @@
             mean = r.stat[j, 1:2, :]
             low_weights = r.wst[j]
             weights = low_weights.astype(f32)
-            raw = nn(r.qc[...], tile) * scale
+            pulls = nn(r.gc[...] if mixed else r.gcb[...], tile)
+            raw = pulls[-own:] * scale
             if mixed:
                 segment = r.stat[j, 2:3, :]
-                pulls = nn(r.gc[...], tile)
                 pull = jnp.zeros_like(weights)
                 level = jnp.zeros_like(weights)
                 for n in range(images):
@@ -490,7 +529,7 @@
                     pull = jnp.where(here, pulls[at], pull)
                     level = jnp.where(here, r.lev[at, :], level)
             else:
-                pull = nn(r.gcb[...], tile)
+                pull = pulls[:own]
                 level = r.levb[...]
             pull = pull * scale
             grad = weights * (pull - level)
@@ -512,9 +551,9 @@
             grads.append((grad * scale).astype(bf16))
         r.dq_sum[...] += nt(side(tiles), side(grads))
 
-    middle_tile = head + (tail - head) // 2 // BIG_UNROLL * BIG_UNROLL
+    step = 2 * BIG_UNROLL
     loop(0, head, partial(backward, True), HEAD_UNROLL)
-    loop(head, middle_tile, partial(backward, False), BIG_UNROLL)
+    loop(head, head + BIG_UNROLL, partial(backward, False), BIG_UNROLL)
     if fused:
         pack_rows = PACK // parts
         mine = pl.ds(pl.multiple_of(place * pack_rows, 16), pack_rows)
@@ -523,16 +562,36 @@
         z_pack = send_z(
             lambda to: r.pack_m.at[pl.ds(pl.multiple_of(to * pack_rows, 16), pack_rows)], lambda s: r.pack_z.at[s - 1]
         )
+    at = head + BIG_UNROLL
+    loop(at, at + step, partial(backward, False), BIG_UNROLL)
+    if fused:
         first_down.wait()
         for b in range(2):
             r.down_1[b] = r.down_1[b] + r.down_c[x * 2 + b]
         second_down = send(r.down_1.at[1 - y], r.down_2, away(2)[1])
-    loop(middle_tile, tail, partial(backward, False), BIG_UNROLL)
-    if fused:
         wait(z_pack)
         r.pack_own[...] = summed(r.pack_m[mine, :], r.pack_z).astype(bf16)
         r.pack_all[core, quad, mine, :] = r.pack_own[...]
         all_pack = send_z(lambda to: r.pack_own, lambda s: r.pack_all.at[core, quad, mine])
+    loop(at + step, at + 2 * step, partial(backward, False), BIG_UNROLL)
+    if fused:
+        wait(all_pack)
+        all_pack = send_quad(lambda q: r.pack_all.at[core, quad], lambda k: r.pack_all.at[core, quad])
+        first_lat.wait()
+        for b in range(2):
+            r.lat_1[b] = r.lat_1[b] + r.lat_c[x * 2 + b]
+        second_lat = send(r.lat_1.at[1 - y], r.lat_2, away(2)[1])
+        first_up.wait()
+        for b in range(2):
+            r.up_1[b] = r.up_1[b] + r.up_c[y * 2 + b]
+        second_up = send(r.up_1.at[1 - x], r.up_2, away(1)[1])
+    loop(at + 2 * step, tail, partial(backward, False), BIG_UNROLL)
+    if fused:
+        second_down.wait()
+        r.down_2[...] = (r.down_1[y].astype(f32) + r.down_2[...].astype(f32)).astype(bf16)
+        z_down = send_z(
+            lambda to: r.down_2.at[pl.ds(pl.multiple_of(to * chunk, 16), chunk)], lambda s: r.down_z.at[s - 1]
+        )
     loop(tail, last, partial(backward, True), HEAD_UNROLL)
 
     dq = r.dq_sum[...].T
@@ -556,83 +615,69 @@
         core_dq.wait()
         r.dq_c[...] = r.dq_c[...] + r.dq_pay[core]
         quad_dq = send_quad(lambda q: r.dq_c.at[q], lambda k: r.dq_q.at[k - 1])
-        wait(out_copies)
-        unit, scale = norm(r.latents[...].astype(f32))
-        r.mid_unit[...] = unit
-        r.mid_scale[...] = scale
-        lat_low = (unit * r.vecs[2:3, :] + r.vecs[3:4, :]).astype(bf16)
-        r.cot_send[...] = lat_low.reshape(parts, own, width)
-        queries = ((nn(lat_low, r.wq[...]) + r.vecs[0:1, :]) * factor).astype(bf16)
-        r.out_send[...] = queries.reshape(parts, own, width)
-        r.qk_all[...] = nt(queries, r.wk[...])
         wait(all_pack)
-        all_pack = send_quad(lambda q: r.pack_all.at[core, quad], lambda k: r.pack_all.at[core, quad])
-        first_up.wait()
-        for b in range(2):
-            r.up_1[b] = r.up_1[b] + r.up_c[y * 2 + b]
-        second_up = send(r.up_1.at[1 - x], r.up_2, away(1)[1])
+        all_pack = send(r.pack_all.at[core], r.pack_all.at[core], mate)
         wait(quad_dq)
         r.dq_own[...] = summed(r.dq_c[quad], r.dq_q).astype(bf16)
         r.dq_all[core, quad, place] = r.dq_own[...]
         z_dq = send_z(lambda to: r.dq_own, lambda s: r.dq_all.at[core, quad, place])
-        second_down.wait()
-        r.down_m[...] = (r.down_1[y].astype(f32) + r.down_2[...].astype(f32)).astype(bf16)
-        z_down = send_z(
-            lambda to: r.down_m.at[pl.ds(pl.multiple_of(to * chunk, 16), chunk)], lambda s: r.down_z.at[s - 1]
-        )
+        all_pack.wait()
+
+        own_cols = pl.ds(pl.multiple_of(lax.rem(group, 8) * LANES, LANES), LANES)
+        lat_cols = pl.ds(pl.multiple_of(place * chunk, LANES), chunk)
+        for d in range(8):
+            r.moment[:, d * LANES : (d + 1) * LANES] = r.pack_all[d % 2, d // 2]
+        order = order_of(264, DQ)
+        wait(out_copies)
+        r.value_out[...] = nt(nn(order[:, :WIDE], r.moment[:WIDE, :]).astype(bf16), r.wo[...])[:FEAT]
+        r.out_out[...] = tn(r.wv[:, lat_cols], r.moment[:WIDE, own_cols])
+        small = r.moment[WIDE : WIDE + 16, :]
+        value_bias = nt(small, r.wo[...])[2:3]
+        small = small.astype(f32)
         wait(z_dq)
         all_dq = send_quad(lambda q: r.dq_all.at[core, quad], lambda k: r.dq_all.at[core, quad])
 
+        second_up.wait()
+        r.up_2[...] = (r.up_1[x].astype(f32) + r.up_2[...].astype(f32)).astype(bf16)
+        z_up = send_z(
+            lambda to: r.up_2.at[pl.ds(pl.multiple_of(to * chunk, 16), chunk)], lambda s: r.up_z.at[s - 1]
+        )
+        second_lat.wait()
+        r.lat_2[...] = (r.lat_1[y].astype(f32) + r.lat_2[...].astype(f32)).astype(bf16)
+        z_lat = send_z(
+            lambda to: r.lat_2.at[pl.ds(pl.multiple_of(to * own, 16), own)], lambda s: r.lat_z.at[s - 1]
+        )
     wait(back_copies)
     r.rgb_out[...] = summed(r.rgb_send[place], r.rgb_back).astype(bf16)
 
     if fused:
+        block = pl.ds(pl.multiple_of(place * chunk, 16), chunk)
+        wait(z_down)
+        r.down_out[...] = summed(r.down_2[block, :], r.down_z)
         wait(all_dq)
         all_dq = send(r.dq_all.at[core], r.dq_all.at[core], mate)
-        wait(all_pack)
-        all_pack = send(r.pack_all.at[core], r.pack_all.at[core], mate)
-        second_up.wait()
-        up_sum = r.up_1[x].astype(f32) + r.up_2[...].astype(f32)
-        r.up_m[...] = up_sum[:width].astype(bf16)
-        z_up = send_z(
-            lambda to: r.up_m.at[pl.ds(pl.multiple_of(to * chunk, 16), chunk)], lambda s: r.up_z.at[s - 1]
-        )
         all_dq.wait()
 
         for z in range(parts):
             for d in range(8):
                 r.dq[(z * 8 + d) * each : (z * 8 + d + 1) * each, :] = r.dq_all[d % 2, d // 2, z]
-        own_cols = pl.ds(pl.multiple_of(lax.rem(group, 8) * LANES, LANES), LANES)
-        lat_cols = pl.ds(pl.multiple_of(place * chunk, LANES), chunk)
         units = r.dq[...].astype(f32)
         lean = units[:, FEAT : FEAT + 1]
         units = jnp.where(lax.broadcasted_iota(jnp.int32, units.shape, 1) < FEAT, units, 0.0)
         gain_sum = jnp.sum(r.qk_all[...] * units, axis=0, keepdims=True)
         bias_sum = jnp.sum(r.qk_all[...] * lean, axis=0, keepdims=True)
         dx = (units * r.feats[0:1, :] + lean * r.feats[1:2, :]).astype(bf16)
-        order = order_of(264, DQ)
-        r.key_out[...] = nn(nt(order, dx).astype(bf16), r.out_send[...].reshape(count, width))[:FEAT]
+        r.key_out[...] = nn(nt(order, dx).astype(bf16), r.branch[...])[:FEAT]
         gq = nn(dx, r.wk[...]) * factor
         gq_low = gq.astype(bf16)
         query_bias = jnp.sum(gq, axis=0, keepdims=True)
         grad_lat = nt(gq_low, r.wq[...])
         latent_gain = jnp.sum(grad_lat * r.mid_unit[...], axis=0, keepdims=True)
         latent_bias = jnp.sum(grad_lat, axis=0, keepdims=True)
-        r.out_send[...] = gq_low.reshape(parts, own, width)
-        r.query_out[...] = tn(
-            r.cot_send[:, :, lat_cols].reshape(count, chunk), r.out_send[:, :, own_cols].reshape(count, LANES)
-        )
+        r.branch[...] = gq_low
+        r.query_out[...] = tn(unfold(place * chunk, chunk), r.branch[:, own_cols])
         r.mid_unit[...] = norm_back(grad_lat * r.vecs[2:3, :], r.mid_unit[...], r.mid_scale[...])
-        r.latents_out[...] = up_sum[width:] + r.mid_unit[rows, own_cols]
-
-        all_pack.wait()
-        for d in range(8):
-            r.moment[:, d * LANES : (d + 1) * LANES] = r.pack_all[d % 2, d // 2]
-        r.value_out[...] = nt(nn(order[:, :WIDE], r.moment[:WIDE, :]).astype(bf16), r.wo[...])[:FEAT]
-        r.out_out[...] = tn(r.wv[:, lat_cols], r.moment[:WIDE, own_cols])
-        small = r.moment[WIDE : WIDE + 16, :]
-        value_bias = nt(small, r.wo[...])[2:3]
-        small = small.astype(f32)
+
         r.vec_out[...] = jnp.concatenate(
             [small[:8], value_bias, query_bias, latent_gain, latent_bias, jnp.zeros((4, width), f32)], axis=0
         )
@@ -641,52 +686,53 @@
         )
         r.ext_out[...] = moved(ends_of, order_of(DQ, DQ), nt)
 
-        block = pl.ds(pl.multiple_of(place * chunk, 16), chunk)
-        wait(z_down)
-        r.down_out[...] = summed(r.down_m[block, :], r.down_z)
         wait(z_up)
-        r.up_out[...] = summed(r.up_m[block, :], r.up_z)
+        r.up_out[...] = summed(r.up_2[block, :], r.up_z)
+        wait(z_lat)
+        r.latents_out[...] = summed(r.lat_2[rows, :], r.lat_z) + r.mid_unit[rows, own_cols]
     else:
         wait(out_copies)
 
 
-def layer(images, slots, parts, fused, sizes, rgb, latents, wq, wo, up, down, wk, wv, cot, vecs):
+def layer(images, slots, parts, fused, sizes, pixel_rgb, latents, wq, wo, up, down, wk, wv, cot, vectors):
     count, width = latents.shape
     own, chunk = count // parts, width // parts
     rows = images * own
     hidden = up.shape[1]
     tiles = slots // TILE
+    colours = (4 * tiles // parts, TILE)
     last = tiles_of(images, slots)[2]
     each = own // 8
     any_, vm = pl.BlockSpec(memory_space=pl.ANY), pl.BlockSpec(memory_space=pltpu.VMEM)
     sds = jax.ShapeDtypeStruct
     V = pltpu.VMEM
     ins = [
-        ("sizes", sizes, pl.BlockSpec(memory_space=pltpu.SMEM)), ("rgb_in", rgb, vm), ("latents", latents, vm),
+        ("sizes", sizes, pl.BlockSpec(memory_space=pltpu.SMEM)), ("pixel_rgb", pixel_rgb, vm), ("latents_h", latents, any_),
         ("wq_h", wq, any_), ("wo_h", wo, any_), ("up_h", up, any_), ("down_h", down, any_),
-        ("wk_in", wk, vm), ("wv_in", wv, vm), ("cot_h", cot, any_), ("vecs", vecs, vm),
-    ]
+        ("wk_in", wk, vm), ("wv_h", wv, any_), ("cot_h", cot, any_),
+    ] + [(f"vec{i}", v, vm) for i, v in enumerate(vectors)]
     pays = [
-        ("down_pay", (2, 4, hidden, LANES), bf16), ("up_pay", (2, 4, width + own, LANES), bf16),
+        ("down_pay", (2, 4, hidden, LANES), bf16), ("up_pay", (2, 4, width, LANES), bf16), ("lat_pay", (2, 4, count, LANES), bf16),
         ("pack", (2, 4, PACK, LANES), bf16), ("dq_pay", (2, 4, each, DQ), bf16),
         ("wk", (DQ, width), bf16), ("wv", (WIDE, width), bf16), ("feats", (8, DQ), f32),
     ]
-    outs = [("out_rows", (parts, own, width), bf16), ("rgb_out", rgb.shape, bf16)]
+    outs = [("out_rows", cot.shape, f32), ("rgb_out", colours, bf16)]
     scratch = [
         ("feat", (last, WIDE, TILE), bf16), ("stat", (last, 8, TILE), f32), ("wst", (last, own, TILE), bf16),
-        ("rgb_recv", (parts - 1,) + rgb.shape, bf16), ("rgbf", (3, tiles, TILE), f32), ("rgbp", (3, tiles, TILE), f32),
-        ("rgb_send", (parts,) + rgb.shape, bf16), ("rgb_back", (parts - 1,) + rgb.shape, bf16),
-        ("wq", wq.shape, bf16), ("wo", wo.shape, bf16), ("up", up.shape, bf16), ("down", down.shape, bf16),
-        ("cot_f", cot.shape, f32), ("cot_send", (parts, own, width), bf16), ("cot_low", (parts, own, width), bf16),
-        ("out_send", (parts, own, width), bf16),
+        ("rgb_in", colours, bf16), ("vecs", (16, width), f32), ("rgb_recv", (parts - 1,) + colours, bf16), ("rgbf", (3, tiles, TILE), f32), ("rgbp", (3, tiles, TILE), f32),
+        ("rgb_send", (parts,) + colours, bf16), ("rgb_back", (parts - 1,) + colours, bf16),
+        ("latents", latents.shape, bf16), ("wv_in", wv.shape, bf16), ("wq", wq.shape, bf16), ("wo", wo.shape, bf16), ("up", up.shape, bf16), ("down", down.shape, bf16),
+        ("cot_f", cot.shape, f32), ("slope", (count, hidden), f32),
+        ("px_send", (images, WIDE, own), bf16), ("px_recv", (parts, WIDE, own), bf16),
+        ("gx_recv", (images, WIDE, own), bf16),
         ("qc", (own, WIDE), bf16), ("qb", (own, 1), f32), ("ext", (images * 16 + 16, own), bf16),
         ("extb", (16, 2 * own), bf16),
-        ("acc", (WIDE, rows), f32), ("acc_big", (WIDE, own), f32), ("unit", (rows, WIDE), f32), ("px", (rows, WIDE), bf16),
+        ("acc", (WIDE, rows), f32), ("acc_big", (WIDE, own), f32), ("unit", (rows, WIDE), f32),
         ("wvo", (WIDE, width), bf16), ("tot", (rows, 1), f32),
-        ("mid_unit", (rows, width), f32), ("mid_scale", (rows, 1), f32),
-        ("act_t", (hidden, rows), bf16), ("mid_t", (width, rows), bf16), ("px_t", (WIDE, rows), bf16),
-        ("gh", (rows, hidden), bf16), ("branch", (rows, width), bf16), ("gx", (rows, WIDE), f32),
-        ("gc", (rows, WIDE), bf16), ("gcb", (own, WIDE), bf16), ("lev", (rows, 1), f32), ("levb", (own, 1), f32),
+        ("mid_unit", (count, width), f32), ("mid_scale", (count, 1), f32),
+        ("act_t", (hidden, count), bf16), ("mid_t", (width, count), bf16), ("px_t", (WIDE, count), bf16),
+        ("branch", (count, width), bf16),
+        ("gc", (rows + own, WIDE), bf16), ("gcb", (2 * own, WIDE), bf16), ("lev", (rows, 1), f32), ("levb", (own, 1), f32),
         ("dq_sum", (WIDE, own), f32),
     ]
     if fused:
@@ -695,12 +741,13 @@
             ("query_out", (chunk, LANES), f32), ("latents_out", (own, LANES), f32), ("key_out", (FEAT, width), f32),
             ("value_out", (FEAT, width), f32), ("vec_out", (16, width), f32), ("ext_out", (8, DQ), f32),
         ]
-        tall = width + own
         scratch += pays + [
             ("down_c", (4, hidden, LANES), bf16), ("down_1", (2, hidden, LANES), bf16), ("down_2", (hidden, LANES), bf16),
-            ("down_m", (hidden, LANES), bf16), ("down_z", (parts - 1, chunk, LANES), bf16),
-            ("up_c", (4, tall, LANES), bf16), ("up_1", (2, tall, LANES), bf16), ("up_2", (tall, LANES), bf16),
-            ("up_m", (width, LANES), bf16), ("up_z", (parts - 1, chunk, LANES), bf16),
+            ("down_z", (parts - 1, chunk, LANES), bf16),
+            ("up_c", (4, width, LANES), bf16), ("up_1", (2, width, LANES), bf16), ("up_2", (width, LANES), bf16),
+            ("lat_c", (4, count, LANES), bf16), ("lat_1", (2, count, LANES), bf16), ("lat_2", (count, LANES), bf16),
+            ("up_z", (parts - 1, chunk, LANES), bf16),
+            ("lat_z", (parts - 1, own, LANES), bf16),
             ("pack_c", (4, PACK, LANES), bf16), ("pack_q", (3, PACK, LANES), bf16), ("pack_m", (PACK, LANES), bf16),
             ("pack_z", (parts - 1, PACK // parts, LANES), bf16), ("pack_own", (PACK // parts, LANES), bf16),
             ("pack_all", (2, 4, PACK, LANES), bf16),
@@ -710,31 +757,28 @@
         ]
     else:
         outs += pays
+        scratch += [("stage0", (2 * own, width), f32), ("stage1", (2 * own, width), f32)]
     names = [n for n, _, _ in ins + outs + scratch] + ["load_sems", "sems"]
     return pl.pallas_call(
         partial(layer_kernel, images, slots, parts, fused, names),
         out_shape=tuple(sds(s, d) for _, s, d in outs),
         in_specs=[spec for _, _, spec in ins],
-        out_specs=(vm,) * len(outs),
+        out_specs=(any_,) + (vm,) * (len(outs) - 1),
         scratch_shapes=[V(s, d) for _, s, d in scratch]
-        + [pltpu.SemaphoreType.DMA((5,)), pltpu.SemaphoreType.DMA((2, SENDS))],
+        + [pltpu.SemaphoreType.DMA((9,)), pltpu.SemaphoreType.DMA((2, SENDS))],
         compiler_params=pltpu.CompilerParams(collective_id=0, has_side_effects=True, vmem_limit_bytes=VMEM_LIMIT),
         name="layer",
     )(*[a for _, a, _ in ins])
 
 
-def finish_kernel(moves, *refs):
-    rows, rgb, vec, ext = refs[:4]
-    whole = refs[4 : 4 + moves]
-    lat_out, rgb_grad = refs[4 + moves : 6 + moves]
-    whole_out = refs[6 + moves : 6 + 2 * moves]
-    vec_out = refs[6 + 2 * moves : -1]
-    sems = refs[-1]
-    copies = [pltpu.make_async_copy(a, b, sems.at[i]) for i, (a, b) in enumerate(zip(whole, whole_out))]
-    for copy in copies:
+def finish_kernel(moves, rgb, vec, ext, *refs):
+    whole, whole_out = refs[:moves], refs[moves : 2 * moves]
+    rgb_grad, *vec_out = refs[2 * moves : -moves - 1]
+    held, sems = refs[-moves - 1 : -1], refs[-1]
+    ins = [pltpu.make_async_copy(a, b, sems.at[0, i]) for i, (a, b) in enumerate(zip(whole, held))]
+    outs = [pltpu.make_async_copy(a, b, sems.at[1, i]) for i, (a, b) in enumerate(zip(held, whole_out))]
+    for copy in ins:
         copy.start()
-    parts, own, width = rows.shape
-    lat_out[0] = rows[...].reshape(parts * own, width).astype(f32)
     colours = rgb[...].astype(f32)
     per = rgb.shape[0] // 4
     rgb_grad[...] = jnp.concatenate(
@@ -748,26 +792,32 @@
         out[...] = vec[i if i < 5 else i + 3, :]
     for i, out in enumerate(vec_out[9:]):
         out[...] = ext[i, :FEAT]
-    wait(copies)
-
-
-def finish(rows, rgb, vec, ext, *whole):
-    parts, own, width = rows.shape
+    for copy, out in zip(ins, outs):
+        copy.wait()
+        out.start()
+    wait(outs)
+
+
+def finish(rgb, vec, ext, *whole):
+    width = vec.shape[1]
     any_, vm = pl.BlockSpec(memory_space=pl.ANY), pl.BlockSpec(memory_space=pltpu.VMEM)
     sds = jax.ShapeDtypeStruct
     n = len(whole)
+    outs = (
+        tuple(sds(a.shape, a.dtype) for a in whole)
+        + (sds((3, rgb.shape[0] // 4 * TILE), bf16),)
+        + (sds((width,), f32),) * 9
+        + (sds((FEAT,), f32),) * 2
+    )
     return pl.pallas_call(
         partial(finish_kernel, n),
-        out_shape=(sds((1, parts * own, width), f32), sds((3, rgb.shape[0] // 4 * TILE), bf16))
-        + tuple(sds(a.shape, a.dtype) for a in whole)
-        + (sds((width,), f32),) * 9
-        + (sds((FEAT,), f32),) * 2,
-        in_specs=[vm] * 4 + [any_] * n,
-        out_specs=(vm,) * 2 + (any_,) * n + (vm,) * 11,
-        scratch_shapes=[pltpu.SemaphoreType.DMA((n,))],
-        compiler_params=pltpu.CompilerParams(vmem_limit_bytes=32 * 2**20),
+        out_shape=outs,
+        in_specs=[vm] * 3 + [any_] * n,
+        out_specs=(any_,) * n + (vm,) * (len(outs) - n),
+        scratch_shapes=[pltpu.VMEM(a.shape, a.dtype) for a in whole] + [pltpu.SemaphoreType.DMA((2, n))],
+        compiler_params=pltpu.CompilerParams(vmem_limit_bytes=VMEM_LIMIT),
         name="finish",
-    )(rows, rgb, vec, ext, *whole)
+    )(rgb, vec, ext, *whole)
 
 
 def restore(rows):
@@ -777,7 +827,7 @@
     )
 
 
-def sums_plain(parts, down_pay, up_pay, pack, dq, latents, wq, wo, wk, wv, vecs, feats):
+def sums_plain(parts, down_pay, up_pay, lat_pay, pack, dq, latents, wq, wo, wk, wv, vecs, feats):
     count, width = latents.shape
     own, chunk = count // parts, width // parts
     place, group, groups = lax.axis_index("pix"), lax.axis_index("dp"), lax.axis_size("dp")
@@ -787,15 +837,15 @@
     def flat(a):
         return a.transpose(2, 1, 0, 3).reshape(a.shape[2], width).astype(f32)
 
-    down_pay = down_pay.reshape(2, 2, 2, *down_pay.shape[2:]).transpose(0, 2, 1, 3, 4).reshape(down_pay.shape)
-
     def scattered(a):
         a = lax.psum_scatter(a, "dp", scatter_dimension=1, tiled=True)
         return lax.psum_scatter(a, "pix", scatter_dimension=0, tiled=True)
 
-    up_all = flat(up_pay)
-    down_total, up_total = scattered(flat(down_pay)), scattered(up_all[:width])
-    latents_sum = lax.psum_scatter(up_all[width:], "dp", scatter_dimension=1, tiled=True)
+    def turned(a):
+        return a.reshape(2, 2, 2, *a.shape[2:]).transpose(0, 2, 1, 3, 4).reshape(a.shape)
+
+    down_total, up_total = scattered(flat(turned(down_pay))), scattered(flat(up_pay))
+    latents_sum = scattered(flat(turned(lat_pay)))
     moment = lax.psum(flat(pack), ("dp", "pix"))
     small, moment = moment[WIDE : WIDE + 8], moment[:WIDE].astype(bf16)
     units = lax.psum(dq.transpose(1, 0, 2, 3).reshape(own, DQ).astype(f32), "dp")
@@ -864,32 +914,26 @@
     parts = lax.axis_size("pix")
     slots = pixel_rgb.shape[1] * parts
     tiles = pixel_rgb.shape[1] // TILE
-    rgb = jnp.pad(pixel_rgb.reshape(3, tiles, TILE), ((0, 1), (0, 0), (0, 0))).reshape(4 * tiles, TILE)
-    fill = lambda v: jnp.pad(v, (0, width - FEAT))
-    none = jnp.zeros((width,), f32)
-    vecs = jnp.stack(
-        [
-            query_bias, out_bias, latent_gain, latent_bias, mlp_gain, mlp_bias, up_bias, down_bias,
-            fill(input_gain), fill(input_bias), value_bias, none, none, none, none, none,
-        ],
-        axis=0,
+    vectors = (
+        query_bias, out_bias, latent_gain, latent_bias, mlp_gain, mlp_bias, up_bias, down_bias,
+        input_gain, input_bias, value_bias,
     )
     fused = lax.axis_size("dp") == 8
     rows, rgb_out, *rest = layer(
-        images, slots, parts, fused, image_sizes, rgb, latents, query_weight, out_weight, up_weight, down_weight,
-        key_weight, value_weight, cotangent, vecs,
+        images, slots, parts, fused, image_sizes, pixel_rgb, latents, query_weight, out_weight, up_weight, down_weight,
+        key_weight, value_weight, cotangent, vectors,
     )
     if fused:
         down, up, out, query, latents_sum, key, value, vec, ext = rest
         (
-            latents_out, rgb_grad, down, up, out, query, latents_sum, key, value,
+            latents_out, down, up, out, query, latents_sum, key, value, rgb_grad,
             db, ub, ob, mg, mb, vb, qb, lg, lb, gain, bias,
-        ) = finish(rows, rgb_out, vec, ext, down, up, out, query, latents_sum, key, value)
+        ) = finish(rgb_out, vec, ext, rows, down, up, out, query, latents_sum, key, value)
     else:
         down, up, out, query, latents_sum, key, value, vec, ext = sums_plain(
-            parts, *rest[:4], latents, query_weight, out_weight, rest[4], rest[5], vecs, rest[6]
+            parts, *rest[:5], latents, query_weight, out_weight, rest[5], rest[6], jnp.stack(vectors[:8]), rest[7]
         )
-        latents_out = rows.reshape(1, latents.shape[0], width).astype(f32)
+        latents_out = rows
         rgb_grad = rgb_out.reshape(4, tiles, TILE)[:3].reshape(3, tiles * TILE)
         db, ub, ob, mg, mb = (vec[i] for i in range(5))
         vb, qb, lg, lb = (vec[i] for i in range(8, 12))

time: 124 us -> 106 us (0.85)
  local copies, waits for them, and re-layouts: 16 us -> 0 us
    unnamed x23 -> x0, local copies, waits for them, and re-layouts: 11.2 us -> none
    pallas_call x1, Pallas kernels: 103 us -> 99.4 us  [layer(): pl.pallas_call(partial(layer_kernel, images, slots, parts, fused, names),...]
    another operation x3 -> x0, local copies, waits for them, and re-layouts: 2.8 us -> none  [shards(): jnp.stack([query_bias, out_bias, latent_gain, latent_bias, mlp_gain, mlp_...]
    pallas_call x1, Pallas kernels: 2.95 us -> 5.49 us  [finish(): pl.pallas_call(partial(finish_kernel, n), out_shape=outs, in_specs=[vm] *...]
    pad x2 -> x0, local copies, waits for them, and re-layouts: 1.37 us -> none  [shards(): fill = lambda v: jnp.pad(v, (0, width - FEAT))]
where the time goes in v3:
time: 106 us
  Pallas kernels  105 us (99%)
    pallas_call x1, Pallas kernels, layer(): pl.pallas_call(partial(layer_kernel, images, slots, parts, fused, names),...  99.4 us
    pallas_call x1, Pallas kernels, finish(): pl.pallas_call(partial(finish_kernel, n), out_shape=outs, in_specs=[vm] *...  5.49 us

profile of v3, /device:TPU:0, one launch (start us, length us, event | category | flops | bytes accessed | tf_op | source)
XLA Modules:
  0.0 105.7 jit_solution(823162303044314348)
XLA Ops:
  0.7 99.4 %layer.1 = (f32[1,512,1024]{2,1,0:T(8,128)}, bf16[32,512]{1,0:T(8,128)(2,1)}, f32[256,128]{1,0:T(8,128)}, f32[256,128]{1,0:T(8,128)}, f32[256,128]{1,0:T(8,128)}...) custom-call(s32[2,4]{1,0:T(2,128)} %refs_0_.1, ...), custom_call_target="tpu_custom_call" | custom-call | tf_op jit(solution)/shard_map/layer/pallas_call | solution.py:762
  100.0 5.5 %finish.1 = (f32[1,512,1024]{2,1,0:T(8,128)}, f32[256,128]{1,0:T(8,128)}, f32[256,128]{1,0:T(8,128)}, f32[256,128]{1,0:T(8,128)}, f32[256,128]{1,0:T(8,128)}, /*...) custom-call(bf16[32,512]{1,0:T(8,128)(2,1)} %get-tuple-element.51.rg, ...), custom_call_target="tpu_custom_call" | custom-call | tf_op jit(solution)/shard_map/finish/pallas_call | solution.py:812

commit v4 on v3

--- a/solution.py
+++ b/solution.py
@@ -127,7 +127,7 @@
 
 
 MLP_UNROLL = 2
-HEAD_UNROLL = 2
+HEAD_UNROLL = 3
 BIG_UNROLL = 3
 
 
@@ -400,6 +400,11 @@
     total_sums, ext_total = None, None
     for blk in range(count // half):
         at = slice(blk * half, (blk + 1) * half)
+        if fused and blk == 1:
+            core_down.wait()
+            for b in range(4):
+                r.down_c[b] = r.down_c[b] + r.down_pay[core, b]
+            first_down = send(r.down_c.at[pl.ds((1 - x) * 2, 2)], r.down_1, away(1)[1])
         grad_down = r.cot_f[0, at, :].astype(bf16)
         grad_hidden = (r.slope[at, :] * nt(grad_down, r.down[...])).astype(bf16)
         fold(blk * half, grad_hidden)
@@ -436,11 +441,6 @@
     for d in range(width // LANES):
         r.pack[d % 2, d // 2, WIDE:, :] = small[:, d * LANES : (d + 1) * LANES]
 
-    if fused:
-        core_down.wait()
-        for b in range(4):
-            r.down_c[b] = r.down_c[b] + r.down_pay[core, b]
-        first_down = send(r.down_c.at[pl.ds((1 - x) * 2, 2)], r.down_1, away(1)[1])
 
     def moments(jj, c):
         cols = pl.ds(pl.multiple_of(jj * 256, 256), 256)
@@ -577,6 +577,30 @@
     if fused:
         wait(all_pack)
         all_pack = send_quad(lambda q: r.pack_all.at[core, quad], lambda k: r.pack_all.at[core, quad])
+    loop(at + 2 * step, tail, partial(backward, False), BIG_UNROLL)
+    loop(tail, last, partial(backward, True), HEAD_UNROLL)
+
+    dq = r.dq_sum[...].T
+    lanes = lax.broadcasted_iota(jnp.int32, dq.shape, 1)
+    gs_sum = dq[:, FEAT : FEAT + 1] + dq[:, FEAT + 1 : FEAT + 2]
+    dq = jnp.where(lanes == FEAT, gs_sum, centred(dq, 1)).astype(bf16)
+    r.dq_pay[...] = jnp.zeros_like(r.dq_pay)
+    each = own // 8
+    for d in range(8):
+        r.dq_pay[d % 2, d // 2, :, :WIDE] = dq[d * each : (d + 1) * each]
+    if fused:
+        core_dq = send(r.dq_pay.at[1 - core], r.dq_c, mate)
+
+    for t in range(parts):
+        r.rgb_send[t] = jnp.concatenate(
+            [r.rgbp[c, t * per : (t + 1) * per, :] for c in range(3)] + [jnp.zeros((per, TILE), f32)], axis=0
+        ).astype(bf16)
+    back_copies = send_z(lambda to: r.rgb_send.at[to], lambda s: r.rgb_back.at[s - 1])
+
+    if fused:
+        core_dq.wait()
+        r.dq_c[...] = r.dq_c[...] + r.dq_pay[core]
+        quad_dq = send_quad(lambda q: r.dq_c.at[q], lambda k: r.dq_q.at[k - 1])
         first_lat.wait()
         for b in range(2):
             r.lat_1[b] = r.lat_1[b] + r.lat_c[x * 2 + b]
@@ -585,42 +609,17 @@
         for b in range(2):
             r.up_1[b] = r.up_1[b] + r.up_c[y * 2 + b]
         second_up = send(r.up_1.at[1 - x], r.up_2, away(1)[1])
-    loop(at + 2 * step, tail, partial(backward, False), BIG_UNROLL)
-    if fused:
-        second_down.wait()
-        r.down_2[...] = (r.down_1[y].astype(f32) + r.down_2[...].astype(f32)).astype(bf16)
-        z_down = send_z(
-            lambda to: r.down_2.at[pl.ds(pl.multiple_of(to * chunk, 16), chunk)], lambda s: r.down_z.at[s - 1]
-        )
-    loop(tail, last, partial(backward, True), HEAD_UNROLL)
-
-    dq = r.dq_sum[...].T
-    lanes = lax.broadcasted_iota(jnp.int32, dq.shape, 1)
-    gs_sum = dq[:, FEAT : FEAT + 1] + dq[:, FEAT + 1 : FEAT + 2]
-    dq = jnp.where(lanes == FEAT, gs_sum, centred(dq, 1)).astype(bf16)
-    r.dq_pay[...] = jnp.zeros_like(r.dq_pay)
-    each = own // 8
-    for d in range(8):
-        r.dq_pay[d % 2, d // 2, :, :WIDE] = dq[d * each : (d + 1) * each]
-    if fused:
-        core_dq = send(r.dq_pay.at[1 - core], r.dq_c, mate)
-
-    for t in range(parts):
-        r.rgb_send[t] = jnp.concatenate(
-            [r.rgbp[c, t * per : (t + 1) * per, :] for c in range(3)] + [jnp.zeros((per, TILE), f32)], axis=0
-        ).astype(bf16)
-    back_copies = send_z(lambda to: r.rgb_send.at[to], lambda s: r.rgb_back.at[s - 1])
-
-    if fused:
-        core_dq.wait()
-        r.dq_c[...] = r.dq_c[...] + r.dq_pay[core]
-        quad_dq = send_quad(lambda q: r.dq_c.at[q], lambda k: r.dq_q.at[k - 1])
         wait(all_pack)
         all_pack = send(r.pack_all.at[core], r.pack_all.at[core], mate)
         wait(quad_dq)
         r.dq_own[...] = summed(r.dq_c[quad], r.dq_q).astype(bf16)
         r.dq_all[core, quad, place] = r.dq_own[...]
         z_dq = send_z(lambda to: r.dq_own, lambda s: r.dq_all.at[core, quad, place])
+        second_down.wait()
+        r.down_2[...] = (r.down_1[y].astype(f32) + r.down_2[...].astype(f32)).astype(bf16)
+        z_down = send_z(
+            lambda to: r.down_2.at[pl.ds(pl.multiple_of(to * chunk, 16), chunk)], lambda s: r.down_z.at[s - 1]
+        )
         all_pack.wait()
 
         own_cols = pl.ds(pl.multiple_of(lax.rem(group, 8) * LANES, LANES), LANES)
@@ -773,12 +772,9 @@
 
 def finish_kernel(moves, rgb, vec, ext, *refs):
     whole, whole_out = refs[:moves], refs[moves : 2 * moves]
-    rgb_grad, *vec_out = refs[2 * moves : -moves - 1]
-    held, sems = refs[-moves - 1 : -1], refs[-1]
-    ins = [pltpu.make_async_copy(a, b, sems.at[0, i]) for i, (a, b) in enumerate(zip(whole, held))]
-    outs = [pltpu.make_async_copy(a, b, sems.at[1, i]) for i, (a, b) in enumerate(zip(held, whole_out))]
-    for copy in ins:
-        copy.start()
+    rgb_grad, *vec_out = refs[2 * moves :]
+    for a, b in zip(whole, whole_out):
+        b[...] = a[...]
     colours = rgb[...].astype(f32)
     per = rgb.shape[0] // 4
     rgb_grad[...] = jnp.concatenate(
@@ -792,15 +788,11 @@
         out[...] = vec[i if i < 5 else i + 3, :]
     for i, out in enumerate(vec_out[9:]):
         out[...] = ext[i, :FEAT]
-    for copy, out in zip(ins, outs):
-        copy.wait()
-        out.start()
-    wait(outs)
 
 
 def finish(rgb, vec, ext, *whole):
     width = vec.shape[1]
-    any_, vm = pl.BlockSpec(memory_space=pl.ANY), pl.BlockSpec(memory_space=pltpu.VMEM)
+    vm = pl.BlockSpec(memory_space=pltpu.VMEM)
     sds = jax.ShapeDtypeStruct
     n = len(whole)
     outs = (
@@ -812,9 +804,8 @@
     return pl.pallas_call(
         partial(finish_kernel, n),
         out_shape=outs,
-        in_specs=[vm] * 3 + [any_] * n,
-        out_specs=(any_,) * n + (vm,) * (len(outs) - n),
-        scratch_shapes=[pltpu.VMEM(a.shape, a.dtype) for a in whole] + [pltpu.SemaphoreType.DMA((2, n))],
+        in_specs=[vm] * (3 + n),
+        out_specs=(vm,) * len(outs),
         compiler_params=pltpu.CompilerParams(vmem_limit_bytes=VMEM_LIMIT),
         name="finish",
     )(rgb, vec, ext, *whole)

time: 106 us -> 103 us (0.972)
  Pallas kernels: 105 us -> 102 us
    pallas_call x1, Pallas kernels: 99.4 us -> 97.3 us  [layer(): pl.pallas_call(partial(layer_kernel, images, slots, parts, fused, names),...]
where the time goes in v4:
time: 103 us
  Pallas kernels  102 us (99%)
    pallas_call x1, Pallas kernels, layer(): pl.pallas_call(partial(layer_kernel, images, slots, parts, fused, names),...  97.3 us
    pallas_call x1, Pallas kernels, finish(): pl.pallas_call(partial(finish_kernel, n), out_shape=outs, in_specs=[vm] *...  4.76 us

profile of v4, /device:TPU:0, one launch (start us, length us, event | category | flops | bytes accessed | tf_op | source)
XLA Modules:
  0.0 103.0 jit_solution(16054397103644334889)
XLA Ops:
  0.7 97.3 %layer.1 = (f32[1,512,1024]{2,1,0:T(8,128)}, bf16[32,512]{1,0:T(8,128)(2,1)}, f32[256,128]{1,0:T(8,128)}, f32[256,128]{1,0:T(8,128)}, f32[256,128]{1,0:T(8,128)}...) custom-call(s32[2,4]{1,0:T(2,128)} %refs_0_.1, ...), custom_call_target="tpu_custom_call" | custom-call | tf_op jit(solution)/shard_map/layer/pallas_call | solution.py:761
  98.0 4.8 %finish.1 = (f32[1,512,1024]{2,1,0:T(8,128)}, f32[256,128]{1,0:T(8,128)}, f32[256,128]{1,0:T(8,128)}, f32[256,128]{1,0:T(8,128)}, f32[256,128]{1,0:T(8,128)}, /*...) custom-call(bf16[32,512]{1,0:T(8,128)(2,1)} %get-tuple-element.51.rg, ...), custom_call_target="tpu_custom_call" | custom-call | tf_op jit(solution)/shard_map/finish/pallas_call | solution.py:804

commit v5 on v4

--- a/solution.py
+++ b/solution.py
@@ -557,26 +557,24 @@
     if fused:
         pack_rows = PACK // parts
         mine = pl.ds(pl.multiple_of(place * pack_rows, 16), pack_rows)
+    at = head + BIG_UNROLL
+    loop(at, at + step, partial(backward, False), BIG_UNROLL)
+    if fused:
         wait(quad_pack)
         r.pack_m[...] = summed(r.pack_c[quad], r.pack_q).astype(bf16)
         z_pack = send_z(
             lambda to: r.pack_m.at[pl.ds(pl.multiple_of(to * pack_rows, 16), pack_rows)], lambda s: r.pack_z.at[s - 1]
         )
-    at = head + BIG_UNROLL
-    loop(at, at + step, partial(backward, False), BIG_UNROLL)
-    if fused:
         first_down.wait()
         for b in range(2):
             r.down_1[b] = r.down_1[b] + r.down_c[x * 2 + b]
         second_down = send(r.down_1.at[1 - y], r.down_2, away(2)[1])
+    loop(at + step, at + 2 * step, partial(backward, False), BIG_UNROLL)
+    if fused:
         wait(z_pack)
         r.pack_own[...] = summed(r.pack_m[mine, :], r.pack_z).astype(bf16)
         r.pack_all[core, quad, mine, :] = r.pack_own[...]
         all_pack = send_z(lambda to: r.pack_own, lambda s: r.pack_all.at[core, quad, mine])
-    loop(at + step, at + 2 * step, partial(backward, False), BIG_UNROLL)
-    if fused:
-        wait(all_pack)
-        all_pack = send_quad(lambda q: r.pack_all.at[core, quad], lambda k: r.pack_all.at[core, quad])
     loop(at + 2 * step, tail, partial(backward, False), BIG_UNROLL)
     loop(tail, last, partial(backward, True), HEAD_UNROLL)
 
@@ -601,6 +599,8 @@
         core_dq.wait()
         r.dq_c[...] = r.dq_c[...] + r.dq_pay[core]
         quad_dq = send_quad(lambda q: r.dq_c.at[q], lambda k: r.dq_q.at[k - 1])
+        wait(all_pack)
+        all_pack = send_quad(lambda q: r.pack_all.at[core, quad], lambda k: r.pack_all.at[core, quad])
         first_lat.wait()
         for b in range(2):
             r.lat_1[b] = r.lat_1[b] + r.lat_c[x * 2 + b]
@@ -609,8 +609,6 @@
         for b in range(2):
             r.up_1[b] = r.up_1[b] + r.up_c[y * 2 + b]
         second_up = send(r.up_1.at[1 - x], r.up_2, away(1)[1])
-        wait(all_pack)
-        all_pack = send(r.pack_all.at[core], r.pack_all.at[core], mate)
         wait(quad_dq)
         r.dq_own[...] = summed(r.dq_c[quad], r.dq_q).astype(bf16)
         r.dq_all[core, quad, place] = r.dq_own[...]
@@ -619,6 +617,21 @@
         r.down_2[...] = (r.down_1[y].astype(f32) + r.down_2[...].astype(f32)).astype(bf16)
         z_down = send_z(
             lambda to: r.down_2.at[pl.ds(pl.multiple_of(to * chunk, 16), chunk)], lambda s: r.down_z.at[s - 1]
+        )
+        wait(all_pack)
+        all_pack = send(r.pack_all.at[core], r.pack_all.at[core], mate)
+        wait(z_dq)
+        all_dq = send_quad(lambda q: r.dq_all.at[core, quad], lambda k: r.dq_all.at[core, quad])
+
+        second_up.wait()
+        r.up_2[...] = (r.up_1[x].astype(f32) + r.up_2[...].astype(f32)).astype(bf16)
+        z_up = send_z(
+            lambda to: r.up_2.at[pl.ds(pl.multiple_of(to * chunk, 16), chunk)], lambda s: r.up_z.at[s - 1]
+        )
+        second_lat.wait()
+        r.lat_2[...] = (r.lat_1[y].astype(f32) + r.lat_2[...].astype(f32)).astype(bf16)
+        z_lat = send_z(
+            lambda to: r.lat_2.at[pl.ds(pl.multiple_of(to * own, 16), own)], lambda s: r.lat_z.at[s - 1]
         )
         all_pack.wait()
 
@@ -633,19 +646,6 @@
         small = r.moment[WIDE : WIDE + 16, :]
         value_bias = nt(small, r.wo[...])[2:3]
         small = small.astype(f32)
-        wait(z_dq)
-        all_dq = send_quad(lambda q: r.dq_all.at[core, quad], lambda k: r.dq_all.at[core, quad])
-
-        second_up.wait()
-        r.up_2[...] = (r.up_1[x].astype(f32) + r.up_2[...].astype(f32)).astype(bf16)
-        z_up = send_z(
-            lambda to: r.up_2.at[pl.ds(pl.multiple_of(to * chunk, 16), chunk)], lambda s: r.up_z.at[s - 1]
-        )
-        second_lat.wait()
-        r.lat_2[...] = (r.lat_1[y].astype(f32) + r.lat_2[...].astype(f32)).astype(bf16)
-        z_lat = send_z(
-            lambda to: r.lat_2.at[pl.ds(pl.multiple_of(to * own, 16), own)], lambda s: r.lat_z.at[s - 1]
-        )
     wait(back_copies)
     r.rgb_out[...] = summed(r.rgb_send[place], r.rgb_back).astype(bf16)
 

time: 103 us -> 103 us (level)
  no operation moved by 1% of the time
where the time goes in v5:
time: 103 us
  Pallas kernels  102 us (99%)
    pallas_call x1, Pallas kernels, layer(): pl.pallas_call(partial(layer_kernel, images, slots, parts, fused, names),...  97 us
    pallas_call x1, Pallas kernels, finish(): pl.pallas_call(partial(finish_kernel, n), out_shape=outs, in_specs=[vm] *...  4.76 us

profile of v5, /device:TPU:0, one launch (start us, length us, event | category | flops | bytes accessed | tf_op | source)
XLA Modules:
  0.0 102.6 jit_solution(4661661745437741384)
XLA Ops:
  0.7 97.0 %layer.1 = (f32[1,512,1024]{2,1,0:T(8,128)}, bf16[32,512]{1,0:T(8,128)(2,1)}, f32[256,128]{1,0:T(8,128)}, f32[256,128]{1,0:T(8,128)}, f32[256,128]{1,0:T(8,128)}...) custom-call(s32[2,4]{1,0:T(2,128)} %refs_0_.1, ...), custom_call_target="tpu_custom_call" | custom-call | tf_op jit(solution)/shard_map/layer/pallas_call | solution.py:761
  97.7 4.8 %finish.1 = (f32[1,512,1024]{2,1,0:T(8,128)}, f32[256,128]{1,0:T(8,128)}, f32[256,128]{1,0:T(8,128)}, f32[256,128]{1,0:T(8,128)}, f32[256,128]{1,0:T(8,128)}, /*...) custom-call(bf16[32,512]{1,0:T(8,128)(2,1)} %get-tuple-element.51.rg, ...), custom_call_target="tpu_custom_call" | custom-call | tf_op jit(solution)/shard_map/finish/pallas_call | solution.py:804
